TPU v7x, 32 devices: a whole 2x2x4 slice. The times are simulated.
32 devices in a mesh: seq: 8 (over z, y), ch: 4 (over x, core).
Axes of the slice: x: 2, y: 2, z: 4, core: 2. Of those that a mesh axis runs over, the one named last changes fastest.
Arguments:
- genome: int32 [2048, 128], P('seq'), may hold values from 0 to 3
- stem_weight: bfloat16 [768, 512], P('ch'), may hold values from -0.5 to 0.5
- dilated_filter_weight: bfloat16 [5, 3, 768, 768], P(None, None, 'ch'), may hold values from -0.125 to 0.125
- head_weight: bfloat16 [768, 5313], P('ch'), may hold values from -0.21875 to 0.21875
- window_start: int32 [128], replicated, may hold values from 0 to 2032
- window_track: int32 [128], replicated, may hold values from 0 to 5312
- targets: float32 [128], replicated, may hold values from 0 to 3
Outputs:
- window_score: float32 [128], replicated
- conv_grad: float32 [5, 3, 768, 768], P(None, None, 'ch', 'seq')
- stem_grad: float32 [768, 512], P('ch')
- head_grad: float32 [768, 5313], P('ch')
Inputs may be any that keep to these rules, and one draw needn't show every extreme that they name: `window_start`: each window lies inside the sequence.
All inputs are finite; a program needn't handle non-finite values.
Results may differ from a plain program's by a relative error of at most 0.0037.
Values may be sent and summed in bfloat16 or wider, within the bound.
No kernel may reach another device: no remote copies, remote signals or barrier semaphores. Data moves between devices by JAX's collectives and lax.ppermute only.
A program may use at most 128 MiB of HBM per device.

v0:
```python
import jax
import jax.numpy as jnp
from jax import lax
from jax.sharding import PartitionSpec as P

LAYERS = 5
WIN = 16


def extended(block, sides, width):
    for axis, dim in sides:
        count = lax.axis_size(axis)
        forward = [(i, i + 1) for i in range(count - 1)]
        backward = [(target, source) for source, target in forward]
        low = lax.ppermute(
            lax.slice_in_dim(block, block.shape[dim] - width, None, axis=dim), axis, forward
        )
        high = lax.ppermute(lax.slice_in_dim(block, 0, width, axis=dim), axis, backward)
        block = jnp.concatenate([low, block, high], axis=dim)
    return block


def passed_along(value, axis, by):
    count = lax.axis_size(axis)
    pairs = [(i, i + by) for i in range(count) if 0 <= i + by < count]
    return lax.ppermute(value, axis, pairs)


def dilations(shard_rows):
    return (shard_rows // 8, shard_rows // 2, shard_rows, 2 * shard_rows, 4 * shard_rows)


def reach_rows(field, distance):
    shard_rows = field.shape[2]
    if distance < shard_rows:
        padded = extended(field, (("seq", 2),), distance)
        return (padded[:, :, :shard_rows], padded[:, :, 2 * distance :])
    hop_count = distance // shard_rows
    lower_rows = passed_along(field, "seq", hop_count)
    upper_rows = passed_along(field, "seq", -hop_count)
    return (lower_rows, upper_rows)


def order_taps(lower_rows, middle, upper_rows):
    forward_taps = jnp.stack([lower_rows[0], middle[0], upper_rows[0]])
    reverse_taps = jnp.stack([upper_rows[1], middle[1], lower_rows[1]])
    return jnp.stack([forward_taps, reverse_taps])


def shards(
    genome, stem_weight, dilated_filter_weight, head_weight, window_start, window_track, targets
):
    shard_rows = genome.shape[0]
    spans = dilations(shard_rows)
    letters = (
        (genome[:, :, None] == jnp.arange(4, dtype=jnp.int32))
        .astype(jnp.bfloat16)
        .reshape(shard_rows, -1)
    )
    strands = jnp.stack([letters, letters[:, ::-1]])
    residual_state = jnp.einsum(
        "sri,ci->scr", strands, stem_weight, preferred_element_type=jnp.float32
    )
    saved_states = []
    stored_taps = []
    for current_layer_index in range(LAYERS):
        active = jax.nn.gelu(residual_state).astype(jnp.bfloat16)
        lower_rows, upper_rows = reach_rows(active, spans[current_layer_index])
        resident_taps = order_taps(lower_rows, active, upper_rows)
        collected_taps = lax.all_gather(resident_taps, "ch", axis=2, tiled=True)
        saved_states.append(residual_state)
        stored_taps.append(collected_taps)
        residual_state = residual_state + jnp.einsum(
            "nezp,efz->nfp",
            collected_taps,
            dilated_filter_weight[current_layer_index],
            preferred_element_type=jnp.float32,
        )
    strand_total = residual_state[0] + residual_state[1]
    first_bin = lax.axis_index("seq") * shard_rows
    positions = first_bin + jnp.arange(shard_rows, dtype=jnp.int32)
    member = (
        (positions[None, :] >= window_start[:, None])
        & (positions[None, :] < window_start[:, None] + WIN)
    ).astype(jnp.float32)
    pooled = jnp.einsum("cr,kr->ck", strand_total, member, precision=lax.Precision.HIGHEST) / WIN
    columns = jnp.take(head_weight, window_track, axis=1).astype(jnp.float32)
    partial_score = 0.5 * jnp.sum(pooled * columns, axis=0)
    window_score = lax.psum(partial_score, ("seq", "ch"))
    counts = jnp.sum((window_track[:, None] == window_track[None, :]).astype(jnp.float32), axis=1)
    loss_slope = (jnp.exp(window_score) - targets) / counts
    window_terms = 0.5 * loss_slope[None, :] * pooled
    weights_back = 0.5 / WIN * loss_slope[None, :] * columns
    back_total = jnp.einsum("ck,kr->cr", weights_back, member, precision=lax.Precision.HIGHEST)
    grad_state = jnp.stack([back_total, back_total])
    layer_gradient_list = []
    for current_layer_index in reversed(range(LAYERS)):
        incoming_gradient = grad_state.astype(jnp.bfloat16)
        weight_part = jnp.einsum(
            "pygj,pij->yig",
            stored_taps[current_layer_index],
            incoming_gradient,
            preferred_element_type=jnp.float32,
        )
        layer_gradient_list.append(weight_part)
        lower_rows, upper_rows = reach_rows(incoming_gradient, spans[current_layer_index])
        back_taps = order_taps(upper_rows, incoming_gradient, lower_rows)
        spread = jnp.einsum(
            "skor,koc->scr",
            back_taps,
            dilated_filter_weight[current_layer_index],
            preferred_element_type=jnp.float32,
        )
        through = lax.psum_scatter(spread, "ch", scatter_dimension=1, tiled=True)
        pullback = jax.vjp(jax.nn.gelu, saved_states[current_layer_index])[1]
        grad_state = grad_state + pullback(through)[0]
    conv_grad = lax.psum_scatter(
        jnp.stack(layer_gradient_list[::-1]), "seq", scatter_dimension=3, tiled=True
    )
    stem_part = jnp.einsum(
        "sri,scr->ci", strands, grad_state.astype(jnp.bfloat16), preferred_element_type=jnp.float32
    )
    head_part = jnp.zeros(head_weight.shape, jnp.float32).at[:, window_track].add(window_terms)
    head_grad, stem_grad = lax.psum((head_part, stem_part), "seq")
    return (window_score, conv_grad, stem_grad, head_grad)


def solution(mesh):
    return jax.shard_map(
        shards,
        mesh=mesh,
        in_specs=(
            P("seq", None),
            P("ch", None),
            P(None, None, "ch", None),
            P("ch", None),
            P(),
            P(),
            P(),
        ),
        out_specs=(P(), P(None, None, "ch", "seq"), P("ch", None), P("ch", None)),
        check_vma=False,
    )
```

profile of v0, /device:TPU:0, one launch (start us, length us, event | category | flops | bytes accessed | tf_op | source)
XLA Modules:
  0.0 853.7 jit_solution(17192382664481940496)
XLA Ops:
  12.1 5.5 collective-permute-start
  21.9 26.7 %all-gather.6.cloned.1.call-done = bf16[2,3,768,256]{3,2,1,0:T(8,128)(2,1)} async-done(((bf16[2,3,192,256]{3,2,1,0:T(8,128)(2,1)}), bf16[2,3,768,256]{3,2,1,0:T(8,128)(2,1)}) %all-gather.6.cloned.1.call-update) | async-done | bytes 2359312 | tf_op jit(solution)/shard_map/all_gather | solution.py:70
  52.6 4.6 collective-permute-start.2
  61.2 25.3 %all-gather.8.cloned.1.call-done = bf16[2,3,768,256]{3,2,1,0:T(8,128)(2,1)} async-done(((bf16[2,3,192,256]{3,2,1,0:T(8,128)(2,1)}), bf16[2,3,768,256]{3,2,1,0:T(8,128)(2,1)}) %all-gather.8.cloned.1.call-update) | async-done | bytes 2359312 | tf_op jit(solution)/shard_map/all_gather | solution.py:70
  90.4 4.6 collective-permute-start.4
  98.1 4.1 collective-permute-done.4
  103.2 24.3 %all-gather.10.cloned.1.call-done = bf16[2,3,768,256]{3,2,1,0:T(8,128)(2,1)} async-done(((bf16[2,3,192,256]{3,2,1,0:T(8,128)(2,1)}), bf16[2,3,768,256]{3,2,1,0:T(8,128)(2,1)}) %all-gather.10.cloned.1.call-update) | async-done | bytes 2359312 | tf_op jit(solution)/shard_map/all_gather | solution.py:70
  138.1 4.1 collective-permute-done.7
  143.3 23.3 %all-gather.12.cloned.1.call-done = bf16[2,3,768,256]{3,2,1,0:T(8,128)(2,1)} async-done(((bf16[2,3,192,256]{3,2,1,0:T(8,128)(2,1)}), bf16[2,3,768,256]{3,2,1,0:T(8,128)(2,1)}) %all-gather.12.cloned.1.call-update) | async-done | bytes 2359312 | tf_op jit(solution)/shard_map/all_gather | solution.py:70
  169.9 4.3 collective-permute-start.8
  178.8 9.2 %collective-permute-done.9 = bf16[2,192,256]{2,1,0:T(8,128)(2,1)S(1)} collective-permute-done((bf16[2,192,256]{2,1,0:T(8,128)(2,1)S(1)}, bf16[2,192,256]{2,1,0:T(8,128)(2,1)S(1)}, u32[]{:S(2)}, u32[]{:S(2)}) %collective-permute-start.9) | collective-permute-done | bytes 196640 | tf_op jit(solution)/shard_map/ppermute | solution.py:26
  189.1 3.7 copy.62
  194.0 16.5 %all-gather.14.cloned.1.call-done = bf16[2,3,768,256]{3,2,1,0:T(8,128)(2,1)} async-done(((bf16[2,3,192,256]{3,2,1,0:T(8,128)(2,1)}), bf16[2,3,768,256]{3,2,1,0:T(8,128)(2,1)}) %all-gather.14.cloned.1.call-update) | async-done | bytes 2359312 | tf_op jit(solution)/shard_map/all_gather | solution.py:70
  213.4 39.4 %psum.21 = f32[128]{0:T(128)S(1)} all-reduce(f32[128]{0:T(128)S(1)} %broadcast_multiply_fusion), channel_id=1, replica_groups=mesh['seq'=8,'ch'=4] {'seq','ch'}, use_global_device_ids=true, to_apply=%region_1.2 | all-reduce | flops 128 | bytes 1024 | tf_op jit(solution)/shard_map/psum | solution.py:89
  254.5 5.5 collective-permute-start.11
  260.0 6.0 collective-permute-done.10
  269.4 31.2 %reduce-scatter.9.cloned.1.call-done = f32[2,192,256]{2,1,0:T(8,128)} async-done(((f32[2,768,256]{2,1,0:T(8,128)}), f32[2,192,256]{2,1,0:T(8,128)}) %reduce-scatter.9.cloned.1.call-update) | async-done | bytes 393232 | tf_op jit(solution)/shard_map/reduce_scatter | solution.py:114
  303.2 4.6 collective-permute-start.13
  315.0 29.3 %reduce-scatter.11.cloned.1.call-done = f32[2,192,256]{2,1,0:T(8,128)} async-done(((f32[2,768,256]{2,1,0:T(8,128)}), f32[2,192,256]{2,1,0:T(8,128)}) %reduce-scatter.11.cloned.1.call-update) | async-done | bytes 393232 | tf_op jit(solution)/shard_map/reduce_scatter | solution.py:114
  346.9 4.7 collective-permute-start.15
  354.1 4.1 collective-permute-done.15
  361.6 28.4 %reduce-scatter.13.cloned.1.call-done = f32[2,192,256]{2,1,0:T(8,128)} async-done(((f32[2,768,256]{2,1,0:T(8,128)}), f32[2,192,256]{2,1,0:T(8,128)}) %reduce-scatter.13.cloned.1.call-update) | async-done | bytes 393232 | tf_op jit(solution)/shard_map/reduce_scatter | solution.py:114
  396.9 4.3 collective-permute-done.16
  404.5 28.3 %reduce-scatter.15.cloned.1.call-done = f32[2,192,256]{2,1,0:T(8,128)} async-done(((f32[2,768,256]{2,1,0:T(8,128)}), f32[2,192,256]{2,1,0:T(8,128)}) %reduce-scatter.15.cloned.1.call-update) | async-done | bytes 393232 | tf_op jit(solution)/shard_map/reduce_scatter | solution.py:114
  439.7 4.3 collective-permute-done.18
  447.6 4.0 scatter_custom_fusion
  451.6 24.1 %reduce-scatter.17.cloned.1.call-done = f32[2,192,256]{2,1,0:T(8,128)} async-done(((f32[2,768,256]{2,1,0:T(8,128)}), f32[2,192,256]{2,1,0:T(8,128)}) %reduce-scatter.17.cloned.1.call-update) | async-done | bytes 393232 | tf_op jit(solution)/shard_map/reduce_scatter | solution.py:114
  491.0 15.3 %copy.96 = f32[5,3,192,768]{2,1,0,3:T(4,128)} copy(f32[5,3,192,768]{3,2,1,0:T(8,128)} %bitcast_dynamic-update-slice_fusion) | data formatting | bytes 17694720
  506.3 18.3 %reshape.110 = f32[768,2880]{1,0:T(8,128)} reshape(f32[768,5,3,192]{3,2,1,0:T(4,128)} %bitcast.244) | data formatting | bytes 17694720
  524.6 156.6 %all-reduce.3.cloned.1.call-done = (f32[192,512]{1,0:T(8,128)}, f32[192,5313]{0,1:T(8,128)}) async-done(((f32[192,512]{1,0:T(8,128)}, f32[192,5313]{0,1:T(8,128)}), (f32[192,512]{1,0:T(8,128)}, f32[192,5313]{0,1:T(8,128)})) %all-reduce.3.cloned.1.call-update) | async-done | bytes 4473616 | tf_op jit(solution)/shard_map/psum | solution.py:124
  681.2 5.7 copy.75
  686.9 154.7 %reduce-scatter.19.cloned.1.call-done = f32[96,2880]{1,0:T(8,128)} async-done(((f32[768,2880]{1,0:T(8,128)}), f32[96,2880]{1,0:T(8,128)}) %reduce-scatter.19.cloned.1.call-update) | async-done | bytes 1105936
  (192 shorter events, 114.1 us)
Async XLA Ops:
  7.2 41.4 %all-gather.6.cloned.1.call-start = ((), (), s32[]{:S(2)}) async-start(), calls=%async_computation.6 | async-start | bytes 2949120 | tf_op jit(solution)/shard_map/all_gather | solution.py:70
  10.8 7.7 collective-permute-start.1
  12.1 8.6 %collective-permute-start = (bf16[2,192,32]{2,1,0:T(8,128)(2,1)S(1)}, bf16[2,192,32]{2,1,0:T(8,128)(2,1)S(1)}, u32[]{:S(2)}, u32[]{:S(2)}) collective-permute-start(bf16[2,192,32]{2,1,0:T(8,128)(2,1)S(1)} %get-tuple-element.89), channel_id=1, source_target_pairs={{0,4},{4,8},{8,12},{12,16},{16,20},{20,24},{24,28},{1,5},{5,9},{9,... | collective-permute-start | bytes 73736 | tf_op jit(solution)/shard_map/ppermute | solution.py:15
  21.8 64.6 %all-gather.8.cloned.1.call-start = ((), (), s32[]{:S(2)}) async-start(), calls=%async_computation.7 | async-start | bytes 2949120 | tf_op jit(solution)/shard_map/all_gather | solution.py:70
  51.3 6.8 collective-permute-start.3
  52.6 7.5 collective-permute-start.2
  61.1 66.3 %all-gather.10.cloned.1.call-start = ((), (), s32[]{:S(2)}) async-start(), calls=%async_computation.8 | async-start | bytes 2949120 | tf_op jit(solution)/shard_map/all_gather | solution.py:70
  89.1 8.9 %collective-permute-start.5 = (bf16[2,192,256]{2,1,0:T(8,128)(2,1)S(1)}, bf16[2,192,256]{2,1,0:T(8,128)(2,1)S(1)}, u32[]{:S(2)}, u32[]{:S(2)}) collective-permute-start(bf16[2,192,256]{2,1,0:T(8,128)(2,1)S(1)} %get-tuple-element.94), channel_id=1, source_target_pairs={{4,0},{8,4},{12,8},{16,12},{20,16},{24,20},{28,24},{5,1},{9,5},{13... | collective-permute-start | bytes 589832 | tf_op jit(solution)/shard_map/ppermute | solution.py:26
  90.4 11.7 %collective-permute-start.4 = (bf16[2,192,256]{2,1,0:T(8,128)(2,1)S(1)}, bf16[2,192,256]{2,1,0:T(8,128)(2,1)S(1)}, u32[]{:S(2)}, u32[]{:S(2)}) collective-permute-start(bf16[2,192,256]{2,1,0:T(8,128)(2,1)S(1)} %get-tuple-element.94), channel_id=1, source_target_pairs={{0,4},{4,8},{8,12},{12,16},{16,20},{20,24},{24,28},{1,5},{5,9},{9,... | collective-permute-start | bytes 589832 | tf_op jit(solution)/shard_map/ppermute | solution.py:26
  103.2 63.4 %all-gather.12.cloned.1.call-start = ((), (), s32[]{:S(2)}) async-start(), calls=%async_computation.9 | async-start | bytes 2949120 | tf_op jit(solution)/shard_map/all_gather | solution.py:70
  130.2 7.9 collective-permute-start.6
  133.6 8.7 %collective-permute-start.7 = (bf16[2,192,256]{2,1,0:T(8,128)(2,1)S(1)}, bf16[2,192,256]{2,1,0:T(8,128)(2,1)S(1)}, u32[]{:S(2)}, u32[]{:S(2)}) collective-permute-start(bf16[2,192,256]{2,1,0:T(8,128)(2,1)S(1)} %get-tuple-element.96), channel_id=1, source_target_pairs={{8,0},{12,4},{16,8},{20,12},{24,16},{28,20},{9,1},{13,5},{17,9},{2... | collective-permute-start | bytes 589832 | tf_op jit(solution)/shard_map/ppermute | solution.py:26
  143.2 67.3 %all-gather.14.cloned.1.call-start = ((), (), s32[]{:S(2)}) async-start(), calls=%async_computation.10 | async-start | bytes 2949120 | tf_op jit(solution)/shard_map/all_gather | solution.py:70
  169.9 8.9 %collective-permute-start.8 = (bf16[2,192,256]{2,1,0:T(8,128)(2,1)S(1)}, bf16[2,192,256]{2,1,0:T(8,128)(2,1)S(1)}, u32[]{:S(2)}, u32[]{:S(2)}) collective-permute-start(bf16[2,192,256]{2,1,0:T(8,128)(2,1)S(1)} %get-tuple-element.98), channel_id=1, source_target_pairs={{0,16},{4,20},{8,24},{12,28},{1,17},{5,21},{9,25},{13,29},{2,18},{... | collective-permute-start | bytes 589832 | tf_op jit(solution)/shard_map/ppermute | solution.py:26
  174.3 13.8 %collective-permute-start.9 = (bf16[2,192,256]{2,1,0:T(8,128)(2,1)S(1)}, bf16[2,192,256]{2,1,0:T(8,128)(2,1)S(1)}, u32[]{:S(2)}, u32[]{:S(2)}) collective-permute-start(bf16[2,192,256]{2,1,0:T(8,128)(2,1)S(1)} %get-tuple-element.98), channel_id=1, source_target_pairs={{16,0},{20,4},{24,8},{28,12},{17,1},{21,5},{25,9},{29,13},{18,2},{... | collective-permute-start | bytes 589832 | tf_op jit(solution)/shard_map/ppermute | solution.py:26
  189.0 111.6 %reduce-scatter.9.cloned.1.call-start = ((), (), s32[]{:S(2)}) async-start(), calls=%async_computation.11 | async-start | bytes 1966080 | tf_op jit(solution)/shard_map/reduce_scatter | solution.py:114
  253.2 12.8 %collective-permute-start.10 = (bf16[2,192,256]{2,1,0:T(8,128)(2,1)S(1)}, bf16[2,192,256]{2,1,0:T(8,128)(2,1)S(1)}, u32[]{:S(2)}, u32[]{:S(2)}) collective-permute-start(bf16[2,192,256]{2,1,0:T(8,128)(2,1)S(1)} %fusion.94), channel_id=1, source_target_pairs={{16,0},{20,4},{24,8},{28,12},{17,1},{21,5},{25,9},{29,13},{18,2},{... | collective-permute-start | bytes 589832 | tf_op jit(solution)/shard_map/ppermute | solution.py:26
  254.5 11.6 %collective-permute-start.11 = (bf16[2,192,256]{2,1,0:T(8,128)(2,1)S(1)}, bf16[2,192,256]{2,1,0:T(8,128)(2,1)S(1)}, u32[]{:S(2)}, u32[]{:S(2)}) collective-permute-start(bf16[2,192,256]{2,1,0:T(8,128)(2,1)S(1)} %fusion.94), channel_id=1, source_target_pairs={{0,16},{4,20},{8,24},{12,28},{1,17},{5,21},{9,25},{13,29},{2,18},{... | collective-permute-start | bytes 589832 | tf_op jit(solution)/shard_map/ppermute | solution.py:26
  269.4 74.9 %reduce-scatter.11.cloned.1.call-start = ((), (), s32[]{:S(2)}) async-start(), calls=%async_computation.12 | async-start | bytes 1966080 | tf_op jit(solution)/shard_map/reduce_scatter | solution.py:114
  301.9 8.5 collective-permute-start.12
  303.2 8.4 collective-permute-start.13
  315.0 75.0 %reduce-scatter.13.cloned.1.call-start = ((), (), s32[]{:S(2)}) async-start(), calls=%async_computation.13 | async-start | bytes 1966080 | tf_op jit(solution)/shard_map/reduce_scatter | solution.py:114
  345.6 8.5 collective-permute-start.14
  346.9 11.3 %collective-permute-start.15 = (bf16[2,192,256]{2,1,0:T(8,128)(2,1)S(1)}, bf16[2,192,256]{2,1,0:T(8,128)(2,1)S(1)}, u32[]{:S(2)}, u32[]{:S(2)}) collective-permute-start(bf16[2,192,256]{2,1,0:T(8,128)(2,1)S(1)} %get-tuple-element.26), channel_id=1, source_target_pairs={{0,4},{4,8},{8,12},{12,16},{16,20},{20,24},{24,28},{1,5},{5,9},{9,... | collective-permute-start | bytes 589832 | tf_op jit(solution)/shard_map/ppermute | solution.py:26
  361.5 71.2 %reduce-scatter.15.cloned.1.call-start = ((), (), s32[]{:S(2)}) async-start(), calls=%async_computation.14 | async-start | bytes 1966080 | tf_op jit(solution)/shard_map/reduce_scatter | solution.py:114
  391.3 5.6 collective-permute-start.17
  394.7 6.5 collective-permute-start.16
  404.4 71.3 %reduce-scatter.17.cloned.1.call-start = ((), (), s32[]{:S(2)}) async-start(), calls=%async_computation.15 | async-start | bytes 1966080 | tf_op jit(solution)/shard_map/reduce_scatter | solution.py:114
  434.1 5.6 collective-permute-start.19
  437.5 6.5 collective-permute-start.18
  447.4 233.8 %all-reduce.3.cloned.1.call-start = ((), (), s32[]{:S(2)}) async-start(), calls=%async_computation.17 | async-start | bytes 11681792 | tf_op jit(solution)/shard_map/psum | solution.py:124
  477.9 363.7 %reduce-scatter.19.cloned.1.call-start = ((), (), s32[]{:S(2)}) async-start(), calls=%async_computation.16 | async-start | bytes 10174464
  (23 other events, 428.1 us)
Sparse Core Ops, SparseCore 0:
  22.0 26.6 all-gather.5
  61.3 25.1 all-gather.7
  103.3 24.1 all-gather.9
  143.3 23.1 all-gather.11
  189.1 21.3 all-gather.13
  269.5 31.1 reduce-scatter.8
  315.1 29.1 reduce-scatter.10
  361.7 28.2 reduce-scatter.12
  404.5 28.1 reduce-scatter.14
  447.5 28.1 reduce-scatter.16
  480.6 200.5 all-reduce.2
  684.8 156.7 reduce-scatter.18
where the time goes:
time: 856 us; the launch traced here: 854 us
  waiting for transfers between devices  628 us (73%)
  starting transfers between devices  57.3 us (7%)
  local copies, waits for them, and re-layouts  55 us (6%)
  matrix products  43.9 us (5%)
  blocking collectives  39.4 us (5%)
  between operations  15.1 us (2%)
  other arithmetic  14.7 us (2%)
    psum x1, waiting for transfers between devices, shards(): head_grad, stem_grad = lax.psum((head_part, stem_part), 'seq')  157 us
    unnamed x13, waiting for transfers between devices  155 us
    reduce_scatter x5, waiting for transfers between devices, shards(): through = lax.psum_scatter(spread, 'ch', scatter_dimension=1, tiled=True)  141 us
    all_gather x5, waiting for transfers between devices, shards(): collected_taps = lax.all_gather(resident_taps, 'ch', axis=2, tiled=True)  116 us
    unnamed x54, local copies, waits for them, and re-layouts  51.6 us
    ppermute x12, waiting for transfers between devices, passed_along(): return lax.ppermute(value, axis, pairs)  43.3 us
    psum x1, blocking collectives, shards(): window_score = lax.psum(partial_score, ('seq', 'ch'))  39.4 us
    ppermute x12, starting transfers between devices, passed_along(): return lax.ppermute(value, axis, pairs)  34.8 us
  transfers between devices with their start and end apart: 32, of which 31 were waited for; matrix products, arithmetic and copies ran while one was open for 7% of the time, Pallas kernels for 0%

commit v1 on v0

v1 whole, which is shorter than its diff:
```python
import jax
import jax.numpy as jnp
from jax import lax
from jax.sharding import PartitionSpec as P

LAYERS = 5
WIN = 16
CORES = 2

bf16 = jnp.bfloat16
f32 = jnp.float32


def dilations(shard_rows):
    return (shard_rows // 8, shard_rows // 2, shard_rows, 2 * shard_rows, 4 * shard_rows)


def core_swap(value):
    count = lax.axis_size("ch")
    return lax.ppermute(value, "ch", [(i, i ^ 1) for i in range(count)])


def chip_shift(value, by):
    count = lax.axis_size("ch")
    return lax.ppermute(value, "ch", [(i, (i + CORES * by) % count) for i in range(count)])


def seq_swap(value, bit):
    count = lax.axis_size("seq")
    return lax.ppermute(value, "seq", [(i, i ^ bit) for i in range(count)])


def choose(index, options):
    picked = options[0]
    for place, option in enumerate(options[1:], 1):
        picked = jnp.where(index == place, option, picked)
    return picked


def rolled(field, by):
    if by == 0:
        return field
    blank = jnp.zeros((abs(by),) + field.shape[1:], field.dtype)
    if by > 0:
        return jnp.concatenate([field[by:], blank], axis=0)
    return jnp.concatenate([blank, field[:by]], axis=0)


def chip_gather(own, chip, chips):
    parts = [own] + [chip_shift(own, by) for by in range(1, chips)]
    return jnp.concatenate(
        [choose((chip - place) % chips, parts) for place in range(chips)], axis=1
    )


def chip_scatter(total, chip, chips):
    parts = jnp.split(total, chips, axis=1)
    mine = choose(chip, parts)
    for by in range(1, chips):
        mine = mine + chip_shift(choose((chip + by) % chips, parts).astype(bf16), by).astype(f32)
    return mine


def seq_scatter(total, seq):
    count = lax.axis_size("seq")
    field = total.reshape((count, total.shape[0] // count) + total.shape[1:])
    bit = 1
    while bit < count:
        pairs = field.reshape((field.shape[0] // 2, 2) + field.shape[1:])
        side = (seq // bit) % 2
        mine = choose(side, [pairs[:, 0], pairs[:, 1]])
        other = choose(side, [pairs[:, 1], pairs[:, 0]]).astype(bf16)
        field = mine + seq_swap(other, bit).astype(f32)
        bit *= 2
    return field[0]


def shards(
    genome, stem_weight, dilated_filter_weight, head_weight, window_start, window_track, targets
):
    shard_rows, pool = genome.shape
    seqs = lax.axis_size("seq")
    chips = lax.axis_size("ch") // CORES
    seq = lax.axis_index("seq")
    strand = lax.axis_index("ch") % CORES
    chip = lax.axis_index("ch") // CORES
    spans = dilations(shard_rows)
    classes = spans[0]
    own_classes = classes // seqs
    steps = shard_rows // classes
    reach = tuple(span // classes * own_classes for span in spans)
    quarter = stem_weight.shape[0]

    sibling_stem = core_swap(stem_weight)
    stem_half = jnp.concatenate(
        [choose(strand, [stem_weight, sibling_stem]), choose(strand, [sibling_stem, stem_weight])]
    )
    stem_parts = [stem_half] + [chip_shift(stem_half, by) for by in range(1, chips)]
    stem_full = jnp.concatenate([choose((chip - p) % chips, stem_parts) for p in range(chips)])

    filters = []
    for layer in range(LAYERS):
        own_filter = dilated_filter_weight[layer]
        sibling_filter = core_swap(own_filter)
        filters.append(
            jnp.concatenate(
                [
                    choose(strand, [own_filter, sibling_filter]),
                    choose(strand, [sibling_filter, own_filter]),
                ],
                axis=1,
            )
        )

    blocks = (
        genome.astype(bf16)
        .reshape(steps, seqs, own_classes, pool)
        .transpose(1, 0, 2, 3)
        .reshape(seqs, steps * own_classes, pool)
    )
    blocks = lax.all_to_all(blocks, "seq", 0, 0, tiled=True)
    bases = blocks.reshape(shard_rows, pool)
    row = jnp.arange(shard_rows, dtype=jnp.int32)
    step_of = row // own_classes
    step_of = jnp.where(strand == 0, step_of, shard_rows // own_classes - 1 - step_of)
    class_of = row % own_classes
    source_row = step_of * own_classes + class_of
    order = (source_row[:, None] == row[None, :]).astype(bf16)
    letter = jnp.arange(4 * pool, dtype=jnp.int32)
    place = jnp.where(strand == 0, letter // 4, pool - 1 - letter // 4)
    spread_place = (jnp.arange(pool, dtype=jnp.int32)[:, None] == place[None, :]).astype(bf16)
    base_of = jnp.where(strand == 0, letter % 4, 3 - letter % 4)
    ordered = jnp.dot(order, bases, preferred_element_type=f32).astype(bf16)
    wide = jnp.dot(ordered, spread_place, preferred_element_type=f32)
    letters = (wide == base_of[None, :].astype(f32)).astype(bf16)
    position = step_of * classes + seq * own_classes + class_of

    member = (
        (position[None, :] >= window_start[:, None])
        & (position[None, :] < window_start[:, None] + WIN)
    ).astype(f32)
    columns = jnp.take(head_weight, window_track, axis=1)
    sibling_columns = core_swap(columns)
    half_columns = jnp.concatenate(
        [choose(strand, [columns, sibling_columns]), choose(strand, [sibling_columns, columns])]
    ).astype(f32)
    counts = jnp.sum((window_track[:, None] == window_track[None, :]).astype(f32), axis=1)

    whole = lax.dot_general(
        letters, stem_full, (((1,), (1,)), ((), ())), preferred_element_type=f32
    )
    active = jax.nn.gelu(whole).astype(bf16)
    stream = choose(chip, jnp.split(whole, chips, axis=1))
    streams = []
    actives = []
    for layer in range(LAYERS):
        streams.append(stream)
        actives.append(active)
        for tap in range(3):
            stream = stream + lax.dot_general(
                rolled(active, (tap - 1) * reach[layer]),
                filters[layer][tap],
                (((1,), (1,)), ((), ())),
                preferred_element_type=f32,
            )
        if layer < LAYERS - 1:
            active = chip_gather(jax.nn.gelu(stream).astype(bf16), chip, chips)

    pooled = (
        lax.dot_general(
            stream, member, (((0,), (1,)), ((), ())), precision=lax.Precision.HIGHEST
        )
        / WIN
    )
    partial_score = 0.5 * jnp.sum(pooled * half_columns, axis=0)
    everyone = seqs * chips * CORES
    scores = lax.all_to_all(
        jnp.broadcast_to(partial_score, (everyone,) + partial_score.shape),
        ("seq", "ch"),
        0,
        0,
        tiled=True,
    )
    window_score = jnp.sum(scores, axis=0)
    loss_slope = (jnp.exp(window_score) - targets) / counts

    pooled_parts = [pooled[:quarter], pooled[quarter:]]
    pooled_own = choose(strand, pooled_parts) + core_swap(choose(1 - strand, pooled_parts))
    bit = 1
    while bit < seqs:
        pooled_own = pooled_own + seq_swap(pooled_own, bit)
        bit *= 2
    head_grad = (
        jnp.zeros(head_weight.shape, f32)
        .at[:, window_track]
        .add(0.5 * loss_slope[None, :] * pooled_own)
    )

    weights_back = 0.5 / WIN * loss_slope[None, :] * half_columns
    grad = lax.dot_general(
        member, weights_back, (((0,), (1,)), ((), ())), precision=lax.Precision.HIGHEST
    )
    filter_grads = []
    for layer in reversed(range(LAYERS)):
        upstream = grad.astype(bf16)
        taps = [rolled(upstream, (1 - tap) * reach[layer]) for tap in range(3)]
        back = sum(
            jnp.dot(taps[tap], filters[layer][tap], preferred_element_type=f32)
            for tap in range(3)
        )
        halves = [
            jnp.concatenate([tap[:, :quarter] for tap in taps], axis=1),
            jnp.concatenate([tap[:, quarter:] for tap in taps], axis=1),
        ]

        def filter_part(half):
            return lax.dot_general(
                actives[layer], half, (((0,), (0,)), ((), ())), preferred_element_type=f32
            )

        theirs = filter_part(choose(1 - strand, halves)).astype(bf16)
        ours = filter_part(choose(strand, halves)) + core_swap(theirs).astype(f32)
        filter_grads.append(seq_scatter(ours, seq))
        through = chip_scatter(back, chip, chips)
        pullback = jax.vjp(jax.nn.gelu, streams[layer])[1]
        grad = grad + pullback(through)[0]

    conv_grad = jnp.stack(
        [g.reshape(g.shape[0], 3, quarter).transpose(1, 2, 0) for g in filter_grads[::-1]]
    )

    stem_part = lax.dot_general(
        grad.astype(bf16), letters, (((0,), (0,)), ((), ())), preferred_element_type=f32
    )
    stem_parts = [stem_part[:quarter], stem_part[quarter:]]
    stem_own = choose(strand, stem_parts) + core_swap(
        choose(1 - strand, stem_parts).astype(bf16)
    ).astype(f32)
    blocks = lax.all_to_all(
        stem_own.astype(bf16).reshape(seqs, quarter // seqs, -1), "seq", 0, 0, tiled=True
    )
    stem_block = jnp.sum(blocks.astype(f32), axis=0)
    stem_grad = lax.all_to_all(
        jnp.broadcast_to(stem_block, (seqs,) + stem_block.shape), "seq", 0, 0, tiled=True
    ).reshape(quarter, -1)
    return (window_score, conv_grad, stem_grad, head_grad)


def solution(mesh):
    return jax.shard_map(
        shards,
        mesh=mesh,
        in_specs=(
            P("seq", None),
            P("ch", None),
            P(None, None, "ch", None),
            P("ch", None),
            P(),
            P(),
            P(),
        ),
        out_specs=(P(), P(None, None, "ch", "seq"), P("ch", None), P("ch", None)),
        check_vma=False,
    )
```

time: 856 us -> 264 us (0.31)
  waiting for transfers between devices: 628 us -> 58.9 us
  blocking collectives: 39.4 us -> 0 us
  other arithmetic: 14.7 us -> 51.5 us
  between operations: 15.1 us -> 2.88 us
  local copies, waits for them, and re-layouts: 55 us -> 44.1 us
    psum x1 -> x0, waiting for transfers between devices: 157 us -> none  [shards(): head_grad, stem_grad = lax.psum((head_part, stem_part), 'seq')]
    unnamed x13 -> x0, waiting for transfers between devices: 155 us -> none
    reduce_scatter x5 -> x0, waiting for transfers between devices: 141 us -> none  [shards(): through = lax.psum_scatter(spread, 'ch', scatter_dimension=1, tiled=True)]
    all_gather x5 -> x0, waiting for transfers between devices: 116 us -> none  [shards(): collected_taps = lax.all_gather(resident_taps, 'ch', axis=2, tiled=True)]
    psum x1 -> x0, blocking collectives: 39.4 us -> none  [shards(): window_score = lax.psum(partial_score, ('seq', 'ch'))]
    unnamed x54 -> x247, local copies, waits for them, and re-layouts: 51.6 us -> 17.5 us
    all_to_all x0 -> x4, starting transfers between devices: none -> 21.1 us  [the longest x1 7.28 us: shards(): blocks = lax.all_to_all(blocks, 'seq', 0, 0, tiled=True)]
    ppermute x20 -> x42, starting transfers between devices: 56.8 us -> 41.7 us  [the longest x18 25.9 us: seq_swap(): return lax.ppermute(value, 'seq', [(i, i ^ bit) for i in range(count)])]
  transfers between devices with their start and end apart: 32 -> 46, of which waited for: 31 -> 16; matrix products, arithmetic and copies ran while one was open for 7% -> 45% of each run, Pallas kernels for 0% -> 0%
where the time goes in v1:
time: 264 us; the launch traced here: 262 us
  starting transfers between devices  62.8 us (24%)
  waiting for transfers between devices  58.9 us (22%)
  other arithmetic  51.5 us (20%)
  local copies, waits for them, and re-layouts  44.1 us (17%)
  matrix products  41.9 us (16%)
  between operations  2.88 us (1%)
    ppermute x10, waiting for transfers between devices, chip_shift(): lax.ppermute(value, 'ch', [(i, (i + CORES * by) % count) for i in range(c...  32 us
    ppermute x18, starting transfers between devices, seq_swap(): return lax.ppermute(value, 'seq', [(i, i ^ bit) for i in range(count)])  25.9 us
    dot_general x10, matrix products, filter_part(): lax.dot_general(actives[layer], half, (((0,), (0,)), ((), ())), preferred...  23.3 us
    ppermute x18, waiting for transfers between devices, seq_swap(): return lax.ppermute(value, 'seq', [(i, i ^ bit) for i in range(count)])  21.7 us
    unnamed x247, local copies, waits for them, and re-layouts  17.5 us
    ppermute x10, starting transfers between devices, chip_shift(): lax.ppermute(value, 'ch', [(i, (i + CORES * by) % count) for i in range(c...  14.1 us
    convert_element_type x15, other arithmetic, seq_scatter(): other = choose(side, [pairs[:, 1], pairs[:, 0]]).astype(bf16)  11.3 us
    add x5, local copies, waits for them, and re-layouts, shards(): ours = filter_part(choose(strand, halves)) + core_swap(theirs).astype(f32)  11.2 us
  transfers between devices with their start and end apart: 46, of which 16 were waited for; matrix products, arithmetic and copies ran while one was open for 45% of the time, Pallas kernels for 0%

profile of v1, /device:TPU:0, one launch (start us, length us, event | category | flops | bytes accessed | tf_op | source)
XLA Modules:
  0.0 262.2 jit_solution(8123622840816719639)
XLA Ops:
  2.2 7.3 %all-to-all-start = ((bf16[8,32,128]{2,1,0:T(8,128)(2,1)}), bf16[8,32,128]{2,1,0:T(8,128)(2,1)}, u32[]{:S(2)}, u32[]{:S(2)}) async-start(bf16[8,32,128]{2,1,0:T(8,128)(2,1)} %copy.228), calls=%async_computation | async-start | bytes 131072 | tf_op jit(solution)/shard_map/all_to_all | solution.py:121
  9.6 4.4 %slice_bitcast_fusion = (bf16[3,192,768]{2,1,0:T(8,128)(2,1)}, bf16[3,192,768]{2,1,0:T(8,128)(2,1)}, bf16[3,192,768]{2,1,0:T(8,128)(2,1)}, bf16[3,192,768]{2,1,0:T(8,128)(2,1)}, bf16[3,192,768]{2,1,0:T(8,128)(2,1)}) fusion(bf16[5,3,192,768]{3,2,1,0:T(8,128)(2,1)} %param.9), kind=kLoop, calls=%fused_computation.81 | loop fusion | bytes 8847360 | tf_op jit(solution)/shard_map/squeeze | solution.py:103
  16.7 10.0 %collective-permute-done.1 = bf16[384,512]{1,0:T(8,128)(2,1)S(1)} collective-permute-done((bf16[384,512]{1,0:T(8,128)(2,1)S(1)}, bf16[384,512]{1,0:T(8,128)(2,1)S(1)}, u32[]{:S(2)}, u32[]{:S(2)}) %collective-permute-start.1) | collective-permute-done | bytes 393248 | tf_op jit(solution)/shard_map/ppermute | solution.py:25
  26.7 3.6 %copy.229 = bf16[192,5313]{0,1:T(8,128)(2,1)S(1)} copy(bf16[192,5313]{1,0:T(8,128)(2,1)} %param.10) | data formatting | bytes 4080384 | tf_op args[3]
  35.6 5.7 %broadcast_select_fusion.1 = (bf16[3,192,768]{2,1,0:T(8,128)(2,1)S(1)}, bf16[3,192,768]{2,1,0:T(8,128)(2,1)S(1)}, bf16[3,192,768]{2,1,0:T(8,128)(2,1)S(1)}, bf16...) fusion(bf16[3,192,768]{2,1,0:T(8,128)(2,1)} %collective-permute, ...), kind=kLoop, calls=%fused_computation.87 | loop fusion | flops 4423680 | bytes 17694720 | tf_op jit(solution)/shard_map/jit(_where)/select_n | solution.py:36
  45.6 5.3 %collective-permute-done.3 = bf16[256,384]{1,0:T(8,128)(2,1)} collective-permute-done((bf16[256,384]{1,0:T(8,128)(2,1)}, bf16[256,384]{1,0:T(8,128)(2,1)}, u32[]{:S(2)}, u32[]{:S(2)}) %collective-permute-start.3) | collective-permute-done | bytes 196640 | tf_op jit(solution)/shard_map/ppermute | solution.py:25
  56.3 4.3 %collective-permute-done.5 = bf16[256,384]{1,0:T(8,128)(2,1)S(1)} collective-permute-done((bf16[256,384]{1,0:T(8,128)(2,1)S(1)}, bf16[256,384]{1,0:T(8,128)(2,1)S(1)}, u32[]{:S(2)}, u32[]{:S(2)}) %collective-permute-start.5) | collective-permute-done | bytes 196640 | tf_op jit(solution)/shard_map/ppermute | solution.py:25
  63.6 4.2 %collective-permute-done.7 = bf16[256,384]{1,0:T(8,128)(2,1)S(1)} collective-permute-done((bf16[256,384]{1,0:T(8,128)(2,1)S(1)}, bf16[256,384]{1,0:T(8,128)(2,1)S(1)}, u32[]{:S(2)}, u32[]{:S(2)}) %collective-permute-start.7) | collective-permute-done | bytes 196640 | tf_op jit(solution)/shard_map/ppermute | solution.py:25
  71.6 3.3 %collective-permute-done.9 = bf16[256,384]{1,0:T(8,128)(2,1)S(1)} collective-permute-done((bf16[256,384]{1,0:T(8,128)(2,1)S(1)}, bf16[256,384]{1,0:T(8,128)(2,1)S(1)}, u32[]{:S(2)}, u32[]{:S(2)}) %collective-permute-start.9) | collective-permute-done | bytes 196640 | tf_op jit(solution)/shard_map/ppermute | solution.py:25
  78.1 6.1 %all-to-all-start.1 = ((f32[32,1,128]{2,1,0:T(1,128)}), f32[32,1,128]{2,1,0:T(1,128)S(1)}, u32[]{:S(2)}, u32[]{:S(2)}) async-start(f32[32,1,128]{2,1,0:T(1,128)} %broadcast_in_dim.21), calls=%async_computation.1 | async-start | bytes 32768 | tf_op jit(solution)/shard_map/all_to_all | solution.py:177
  85.9 5.3 %all-to-all-done.1 = f32[32,1,128]{2,1,0:T(1,128)S(1)} async-done(((f32[32,1,128]{2,1,0:T(1,128)}), f32[32,1,128]{2,1,0:T(1,128)S(1)}, u32[]{:S(2)}, u32[]{:S(2)}) %all-to-all-start.1) | async-done | bytes 16416 | tf_op jit(solution)/shard_map/all_to_all | solution.py:177
  108.6 4.4 %collective-permute-done.41 = f32[192,128]{1,0:T(8,128)S(1)} collective-permute-done((f32[192,128]{1,0:T(8,128)S(1)}, f32[192,128]{1,0:T(8,128)S(1)}, u32[]{:S(2)}, u32[]{:S(2)}) %collective-permute-start.41) | collective-permute-done | bytes 98336 | tf_op jit(solution)/shard_map/ppermute | solution.py:30
  113.8 4.3 %scatter_custom_fusion = f32[192,5313]{0,1:T(8,128)} fusion(s32[128]{0:T(128)} %copy-done.116, f32[128,192]{1,0:T(8,128)} %copy.274, f32[]{:T(128)} %constant.275.clone.1), kind=kCustom, calls=%fused_computation.2 | custom fusion | flops 24576 | bytes 4080896 | tf_op jit(solution)/shard_map/scatter-add | solution.py:196
  118.1 5.7 %copy.275 = f32[192,5313]{1,0:T(8,128)} copy(f32[192,5313]{0,1:T(8,128)} %scatter_custom_fusion) | data formatting | bytes 8160768
  137.7 2.5 collective-permute-done.15
  148.2 3.0 %convert_add_fusion = f32[768,576]{0,1:T(8,128)} fusion(bf16[768,576]{0,1:T(8,128)(2,1)} %collective-permute-done.32, pred[]{:T(512)S(6)} %eq.90, bf16[256,384]{1,0:T(8,128)(2,1)S(1)} %copy-done.27, bf16[256,384]{1,0:T(8,128)(2,1)S(1)} %copy-done.30, bf16[256,192]{1,0:T(8,128)(2,1)S(1)} %copy-done.88, bf16[256,192]{1,0:T(8,128)(2,1)S(1)} %copy-done.84, ...), kind=kOutput, calls=%fused_computation.28 | convolution fusion | flops 230080512 | bytes 3637249 | tf_op jit(solution)/shard_map/dot_general | solution.py:217
  158.3 3.0 %convert_add_fusion.1 = f32[768,576]{0,1:T(8,128)} fusion(bf16[768,576]{0,1:T(8,128)(2,1)} %collective-permute-done.28, pred[]{:T(512)S(6)} %eq.90, bf16[256,384]{1,0:T(8,128)(2,1)S(1)} %copy-done.41, bf16[256,384]{1,0:T(8,128)(2,1)S(1)} %copy-done.43, bf16[256,192]{1,0:T(8,128)(2,1)S(1)} %copy-done.58, bf16[256,192]{1,0:T(8,128)(2,1)S(1)} %copy-done.96, ...), kind=kOutput, calls=%fused_computation.29 | convolution fusion | flops 230080512 | bytes 3637249 | tf_op jit(solution)/shard_map/dot_general | solution.py:217
  166.9 3.7 %all-to-all-start.2 = ((bf16[8,24,512]{2,1,0:T(8,128)(2,1)}), bf16[8,24,512]{2,1,0:T(8,128)(2,1)S(1)}, u32[]{:S(2)}, u32[]{:S(2)}) async-start(bf16[8,24,512]{2,1,0:T(8,128)(2,1)} %bitcast.101), calls=%async_computation.2 | async-start | bytes 393216 | tf_op jit(solution)/shard_map/all_to_all | solution.py:239
  170.6 3.4 %convert_add_fusion.2 = f32[768,576]{0,1:T(8,128)} fusion(bf16[768,576]{0,1:T(8,128)(2,1)} %collective-permute-done.24, pred[]{:T(512)S(6)} %eq.90, bf16[256,384]{1,0:T(8,128)(2,1)S(1)} %copy-done.37, bf16[256,384]{1,0:T(8,128)(2,1)S(1)} %copy-done.39, bf16[256,192]{1,0:T(8,128)(2,1)} %copy-done.78, bf16[256,192]{1,0:T(8,128)(2,1)} %copy-done.100, ...), kind=kOutput, calls=%fused_computation.30 | convolution fusion | flops 230080512 | bytes 3637249 | tf_op jit(solution)/shard_map/dot_general | solution.py:217
  183.4 3.0 %convert_add_fusion.3 = f32[768,576]{0,1:T(8,128)} fusion(bf16[768,576]{0,1:T(8,128)(2,1)} %collective-permute-done.20, pred[]{:T(512)S(6)} %eq.90, bf16[256,384]{1,0:T(8,128)(2,1)S(1)} %copy-done.33, bf16[256,384]{1,0:T(8,128)(2,1)S(1)} %copy-done.35, bf16[256,192]{1,0:T(8,128)(2,1)S(1)} %copy-done.71, bf16[256,192]{1,0:T(8,128)(2,1)S(1)} %copy-done.104, ...), kind=kOutput, calls=%fused_computation.31 | convolution fusion | flops 230080512 | bytes 3637249 | tf_op jit(solution)/shard_map/dot_general | solution.py:217
  186.5 2.8 %copy.238 = f32[768,576]{1,0:T(8,128)} copy(f32[768,576]{0,1:T(8,128)} %convert_add_fusion.3) | data formatting | bytes 3538944 | tf_op jit(solution)/shard_map/add | solution.py:222
  189.3 2.4 fusion.52
  197.6 2.6 collective-permute-start.35
  201.1 4.1 %all-to-all-start.3 = ((f32[8,24,512]{2,1,0:T(8,128)}), f32[8,24,512]{2,1,0:T(8,128)}, u32[]{:S(2)}, u32[]{:S(2)}) async-start(f32[8,24,512]{2,1,0:T(8,128)} %broadcast_in_dim.22), calls=%async_computation.3 | async-start | bytes 786432 | tf_op jit(solution)/shard_map/all_to_all | solution.py:243
  208.8 3.4 %convert_add_fusion.4 = f32[768,576]{0,1:T(8,128)} fusion(bf16[768,576]{0,1:T(8,128)(2,1)} %collective-permute-done.16, bf16[256,768]{1,0:T(8,128)(2,1)S(1)} %copy-done.17, pred[]{:T(512)S(6)} %eq.90, bf16[256,192]{1,0:T(8,128)(2,1)} %copy-done.65, bf16[256,192]{1,0:T(8,128)(2,1)} %copy-done.98, bf16[256,192]{1,0:T(8,128)(2,1)} %copy-done.67, ...), kind=kOutput, calls=%fused_computation.32 | convolution fusion | flops 229294080 | bytes 3637249 | tf_op jit(solution)/shard_map/dot_general | solution.py:217
  212.2 2.8 %copy.232 = f32[768,576]{1,0:T(8,128)} copy(f32[768,576]{0,1:T(8,128)} %convert_add_fusion.4) | data formatting | bytes 3538944 | tf_op jit(solution)/shard_map/add | solution.py:222
  215.0 2.4 fusion.51
  221.8 2.5 collective-permute-start.31
  225.0 2.9 %collective-permute-start.26 = (bf16[2,96,576]{2,1,0:T(8,128)(2,1)}, bf16[2,96,576]{2,1,0:T(8,128)(2,1)S(1)}, u32[]{:S(2)}, u32[]{:S(2)}) collective-permute-start(bf16[2,96,576]{2,1,0:T(8,128)(2,1)} %fusion.146), channel_id=1, source_target_pairs={{0,8},{4,12},{8,0},{12,4},{16,24},{20,28},{24,16},{28,20},{1,9},{5... | collective-permute-start | bytes 663560 | tf_op jit(solution)/shard_map/ppermute | solution.py:30
  229.4 3.6 %collective-permute-done.26 = bf16[2,96,576]{2,1,0:T(8,128)(2,1)S(1)} collective-permute-done((bf16[2,96,576]{2,1,0:T(8,128)(2,1)}, bf16[2,96,576]{2,1,0:T(8,128)(2,1)S(1)}, u32[]{:S(2)}, u32[]{:S(2)}) %collective-permute-start.26) | collective-permute-done | bytes 221216 | tf_op jit(solution)/shard_map/ppermute | solution.py:30
  247.4 3.4 %collective-permute-done.18 = bf16[2,96,576]{2,1,0:T(8,128)(2,1)S(1)} collective-permute-done((bf16[2,96,576]{2,1,0:T(8,128)(2,1)S(1)}, bf16[2,96,576]{2,1,0:T(8,128)(2,1)S(1)}, u32[]{:S(2)}, u32[]{:S(2)}) %collective-permute-start.18) | collective-permute-done | bytes 221216 | tf_op jit(solution)/shard_map/ppermute | solution.py:30
  254.9 4.2 %collective-permute-done.19 = bf16[1,96,576]{2,1,0:T(8,128)(2,1)S(1)} collective-permute-done((bf16[1,96,576]{2,1,0:T(8,128)(2,1)S(1)}, bf16[1,96,576]{2,1,0:T(8,128)(2,1)S(1)}, u32[]{:S(2)}, u32[]{:S(2)}) %collective-permute-start.19) | collective-permute-done | bytes 110624 | tf_op jit(solution)/shard_map/ppermute | solution.py:30
  (467 shorter events, 129.9 us)
Async XLA Ops:
  2.2 31.2 %all-to-all-start = ((bf16[8,32,128]{2,1,0:T(8,128)(2,1)}), bf16[8,32,128]{2,1,0:T(8,128)(2,1)}, u32[]{:S(2)}, u32[]{:S(2)}) async-start(bf16[8,32,128]{2,1,0:T(8,128)(2,1)} %copy.228), calls=%async_computation | async-start | bytes 131072 | tf_op jit(solution)/shard_map/all_to_all | solution.py:121
  14.0 21.5 %collective-permute-start.10 = (bf16[3,192,768]{2,1,0:T(8,128)(2,1)}, bf16[3,192,768]{2,1,0:T(8,128)(2,1)}, u32[]{:S(2)}, u32[]{:S(2)}) collective-permute-start(bf16[3,192,768]{2,1,0:T(8,128)(2,1)} %get-tuple-element.56), channel_id=1, source_target_pairs={{0,1},{1,0},{2,3},{3,2},{4,5},{5,4},{6,7},{7,6},{8,9},{9,8},{10,11... | collective-permute-start | bytes 2654216 | tf_op jit(solution)/shard_map/ppermute | solution.py:20
  14.4 21.1 %collective-permute-start.2 = (bf16[3,192,768]{2,1,0:T(8,128)(2,1)}, bf16[3,192,768]{2,1,0:T(8,128)(2,1)}, u32[]{:S(2)}, u32[]{:S(2)}) collective-permute-start(bf16[3,192,768]{2,1,0:T(8,128)(2,1)} %get-tuple-element.59), channel_id=1, source_target_pairs={{0,1},{1,0},{2,3},{3,2},{4,5},{5,4},{6,7},{7,6},{8,9},{9,8},{10,11... | collective-permute-start | bytes 2654216 | tf_op jit(solution)/shard_map/ppermute | solution.py:20
  14.5 21.0 %collective-permute-start.4 = (bf16[3,192,768]{2,1,0:T(8,128)(2,1)}, bf16[3,192,768]{2,1,0:T(8,128)(2,1)}, u32[]{:S(2)}, u32[]{:S(2)}) collective-permute-start(bf16[3,192,768]{2,1,0:T(8,128)(2,1)} %get-tuple-element.58), channel_id=1, source_target_pairs={{0,1},{1,0},{2,3},{3,2},{4,5},{5,4},{6,7},{7,6},{8,9},{9,8},{10,11... | collective-permute-start | bytes 2654216 | tf_op jit(solution)/shard_map/ppermute | solution.py:20
  15.0 20.6 %collective-permute-start.6 = (bf16[3,192,768]{2,1,0:T(8,128)(2,1)}, bf16[3,192,768]{2,1,0:T(8,128)(2,1)}, u32[]{:S(2)}, u32[]{:S(2)}) collective-permute-start(bf16[3,192,768]{2,1,0:T(8,128)(2,1)} %get-tuple-element.57), channel_id=1, source_target_pairs={{0,1},{1,0},{2,3},{3,2},{4,5},{5,4},{6,7},{7,6},{8,9},{9,8},{10,11... | collective-permute-start | bytes 2654216 | tf_op jit(solution)/shard_map/ppermute | solution.py:20
  15.1 11.5 %collective-permute-start.1 = (bf16[384,512]{1,0:T(8,128)(2,1)S(1)}, bf16[384,512]{1,0:T(8,128)(2,1)S(1)}, u32[]{:S(2)}, u32[]{:S(2)}) collective-permute-start(bf16[384,512]{1,0:T(8,128)(2,1)S(1)} %pad_maximum_fusion.9), channel_id=1, source_target_pairs={{0,2},{1,3},{2,0},{3,1},{4,6},{5,7},{6,4},{7,5},{8,10},{9,11},{10,... | collective-permute-start | bytes 1179656 | tf_op jit(solution)/shard_map/ppermute | solution.py:25
  26.7 8.9 %collective-permute-start.8 = (bf16[3,192,768]{2,1,0:T(8,128)(2,1)}, bf16[3,192,768]{2,1,0:T(8,128)(2,1)}, u32[]{:S(2)}, u32[]{:S(2)}) collective-permute-start(bf16[3,192,768]{2,1,0:T(8,128)(2,1)} %get-tuple-element.60), channel_id=1, source_target_pairs={{0,1},{1,0},{2,3},{3,2},{4,5},{5,4},{6,7},{7,6},{8,9},{9,8},{10,11... | collective-permute-start | bytes 2654216 | tf_op jit(solution)/shard_map/ppermute | solution.py:20
  43.3 7.6 %collective-permute-start.3 = (bf16[256,384]{1,0:T(8,128)(2,1)}, bf16[256,384]{1,0:T(8,128)(2,1)}, u32[]{:S(2)}, u32[]{:S(2)}) collective-permute-start(bf16[256,384]{1,0:T(8,128)(2,1)} %get-tuple-element.127), channel_id=1, source_target_pairs={{0,2},{1,3},{2,0},{3,1},{4,6},{5,7},{6,4},{7,5},{8,10},{9,11},{10,... | collective-permute-start | bytes 589832 | tf_op jit(solution)/shard_map/ppermute | solution.py:25
  45.4 25.3 %collective-permute-start.11 = (bf16[192,128]{1,0:T(8,128)(2,1)}, bf16[192,128]{1,0:T(8,128)(2,1)}, u32[]{:S(2)}, u32[]{:S(2)}) collective-permute-start(bf16[192,128]{1,0:T(8,128)(2,1)} %select_bitcast_fusion), channel_id=1, source_target_pairs={{0,1},{1,0},{2,3},{3,2},{4,5},{5,4},{6,7},{7,6},{8,9},{9,8},{10,11... | collective-permute-start | bytes 147464 | tf_op jit(solution)/shard_map/ppermute | solution.py:20
  78.1 13.1 %all-to-all-start.1 = ((f32[32,1,128]{2,1,0:T(1,128)}), f32[32,1,128]{2,1,0:T(1,128)S(1)}, u32[]{:S(2)}, u32[]{:S(2)}) async-start(f32[32,1,128]{2,1,0:T(1,128)} %broadcast_in_dim.21), calls=%async_computation.1 | async-start | bytes 32768 | tf_op jit(solution)/shard_map/all_to_all | solution.py:177
  85.8 10.1 %collective-permute-start.38 = (f32[192,128]{1,0:T(8,128)}, f32[192,128]{1,0:T(8,128)}, u32[]{:S(2)}, u32[]{:S(2)}) collective-permute-start(f32[192,128]{1,0:T(8,128)} %slice_select_fusion.2), channel_id=1, source_target_pairs={{0,1},{1,0},{2,3},{3,2},{4,5},{5,4},{6,7},{7,6},{8,9},{9,8},{10,11... | collective-permute-start | bytes 294920 | tf_op jit(solution)/shard_map/ppermute | solution.py:20
  99.2 47.6 %collective-permute-start.32 = (bf16[768,576]{0,1:T(8,128)(2,1)}, bf16[768,576]{0,1:T(8,128)(2,1)}, u32[]{:S(2)}, u32[]{:S(2)}) collective-permute-start(bf16[768,576]{0,1:T(8,128)(2,1)} %convolution_convert_fusion), channel_id=1, source_target_pairs={{0,1},{1,0},{2,3},{3,2},{4,5},{5,4},{6,7},{7,6},{8,9},{9,8},{10,11... | collective-permute-start | bytes 2654216 | tf_op jit(solution)/shard_map/ppermute | solution.py:20
  104.7 19.1 %collective-permute-start.13 = (bf16[256,384]{1,0:T(8,128)(2,1)}, bf16[256,384]{1,0:T(8,128)(2,1)}, u32[]{:S(2)}, u32[]{:S(2)}) collective-permute-start(bf16[256,384]{1,0:T(8,128)(2,1)} %select_convert_fusion.14), channel_id=1, source_target_pairs={{0,2},{1,3},{2,0},{3,1},{4,6},{5,7},{6,4},{7,5},{8,10},{9,11},{10,... | collective-permute-start | bytes 589832 | tf_op jit(solution)/shard_map/ppermute | solution.py:25
  108.6 49.5 %collective-permute-start.28 = (bf16[768,576]{0,1:T(8,128)(2,1)}, bf16[768,576]{0,1:T(8,128)(2,1)}, u32[]{:S(2)}, u32[]{:S(2)}) collective-permute-start(bf16[768,576]{0,1:T(8,128)(2,1)} %convolution_convert_fusion.1), channel_id=1, source_target_pairs={{0,1},{1,0},{2,3},{3,2},{4,5},{5,4},{6,7},{7,6},{8,9},{9,8},{10,11... | collective-permute-start | bytes 2654216 | tf_op jit(solution)/shard_map/ppermute | solution.py:20
  130.7 39.9 %collective-permute-start.24 = (bf16[768,576]{0,1:T(8,128)(2,1)}, bf16[768,576]{0,1:T(8,128)(2,1)}, u32[]{:S(2)}, u32[]{:S(2)}) collective-permute-start(bf16[768,576]{0,1:T(8,128)(2,1)} %convolution_convert_fusion.2), channel_id=1, source_target_pairs={{0,1},{1,0},{2,3},{3,2},{4,5},{5,4},{6,7},{7,6},{8,9},{9,8},{10,11... | collective-permute-start | bytes 2654216 | tf_op jit(solution)/shard_map/ppermute | solution.py:20
  137.7 45.7 %collective-permute-start.20 = (bf16[768,576]{0,1:T(8,128)(2,1)}, bf16[768,576]{0,1:T(8,128)(2,1)}, u32[]{:S(2)}, u32[]{:S(2)}) collective-permute-start(bf16[768,576]{0,1:T(8,128)(2,1)} %convolution_convert_fusion.3), channel_id=1, source_target_pairs={{0,1},{1,0},{2,3},{3,2},{4,5},{5,4},{6,7},{7,6},{8,9},{9,8},{10,11... | collective-permute-start | bytes 2654216 | tf_op jit(solution)/shard_map/ppermute | solution.py:20
  144.2 64.6 %collective-permute-start.16 = (bf16[768,576]{0,1:T(8,128)(2,1)}, bf16[768,576]{0,1:T(8,128)(2,1)}, u32[]{:S(2)}, u32[]{:S(2)}) collective-permute-start(bf16[768,576]{0,1:T(8,128)(2,1)} %convolution_convert_fusion.4), channel_id=1, source_target_pairs={{0,1},{1,0},{2,3},{3,2},{4,5},{5,4},{6,7},{7,6},{8,9},{9,8},{10,11... | collective-permute-start | bytes 2654216 | tf_op jit(solution)/shard_map/ppermute | solution.py:20
  146.7 7.6 %collective-permute-start.36 = (bf16[256,384]{1,0:T(8,128)(2,1)}, bf16[256,384]{1,0:T(8,128)(2,1)}, u32[]{:S(2)}, u32[]{:S(2)}) collective-permute-start(bf16[256,384]{1,0:T(8,128)(2,1)} %select_convert_fusion.11), channel_id=1, source_target_pairs={{0,2},{1,3},{2,0},{3,1},{4,6},{5,7},{6,4},{7,5},{8,10},{9,11},{10,... | collective-permute-start | bytes 589832 | tf_op jit(solution)/shard_map/ppermute | solution.py:25
  154.3 24.1 %collective-permute-start.33 = (bf16[4,96,576]{2,1,0:T(8,128)(2,1)}, bf16[4,96,576]{2,1,0:T(8,128)(2,1)}, u32[]{:S(2)}, u32[]{:S(2)}) collective-permute-start(bf16[4,96,576]{2,1,0:T(8,128)(2,1)} %fusion.55), channel_id=1, source_target_pairs={{0,4},{4,0},{8,12},{12,8},{16,20},{20,16},{24,28},{28,24},{1,5},{5... | collective-permute-start | bytes 1327112 | tf_op jit(solution)/shard_map/ppermute | solution.py:30
  164.1 28.1 %collective-permute-start.29 = (bf16[4,96,576]{2,1,0:T(8,128)(2,1)}, bf16[4,96,576]{2,1,0:T(8,128)(2,1)}, u32[]{:S(2)}, u32[]{:S(2)}) collective-permute-start(bf16[4,96,576]{2,1,0:T(8,128)(2,1)} %fusion.54), channel_id=1, source_target_pairs={{0,4},{4,0},{8,12},{12,8},{16,20},{20,16},{24,28},{28,24},{1,5},{5... | collective-permute-start | bytes 1327112 | tf_op jit(solution)/shard_map/ppermute | solution.py:30
  166.9 33.3 %all-to-all-start.2 = ((bf16[8,24,512]{2,1,0:T(8,128)(2,1)}), bf16[8,24,512]{2,1,0:T(8,128)(2,1)S(1)}, u32[]{:S(2)}, u32[]{:S(2)}) async-start(bf16[8,24,512]{2,1,0:T(8,128)(2,1)} %bitcast.101), calls=%async_computation.2 | async-start | bytes 393216 | tf_op jit(solution)/shard_map/all_to_all | solution.py:239
  176.7 42.6 %collective-permute-start.25 = (bf16[4,96,576]{2,1,0:T(8,128)(2,1)}, bf16[4,96,576]{2,1,0:T(8,128)(2,1)}, u32[]{:S(2)}, u32[]{:S(2)}) collective-permute-start(bf16[4,96,576]{2,1,0:T(8,128)(2,1)} %fusion.53), channel_id=1, source_target_pairs={{0,4},{4,0},{8,12},{12,8},{16,20},{20,16},{24,28},{28,24},{1,5},{5... | collective-permute-start | bytes 1327112 | tf_op jit(solution)/shard_map/ppermute | solution.py:30
  181.9 13.3 %collective-permute-start.34 = (bf16[2,96,576]{2,1,0:T(8,128)(2,1)}, bf16[2,96,576]{2,1,0:T(8,128)(2,1)}, u32[]{:S(2)}, u32[]{:S(2)}) collective-permute-start(bf16[2,96,576]{2,1,0:T(8,128)(2,1)} %fusion.148), channel_id=1, source_target_pairs={{0,8},{4,12},{8,0},{12,4},{16,24},{20,28},{24,16},{28,20},{1,9},{5... | collective-permute-start | bytes 663560 | tf_op jit(solution)/shard_map/ppermute | solution.py:30
  191.7 36.4 %collective-permute-start.21 = (bf16[4,96,576]{2,1,0:T(8,128)(2,1)}, bf16[4,96,576]{2,1,0:T(8,128)(2,1)}, u32[]{:S(2)}, u32[]{:S(2)}) collective-permute-start(bf16[4,96,576]{2,1,0:T(8,128)(2,1)} %fusion.52), channel_id=1, source_target_pairs={{0,4},{4,0},{8,12},{12,8},{16,20},{20,16},{24,28},{28,24},{1,5},{5... | collective-permute-start | bytes 1327112 | tf_op jit(solution)/shard_map/ppermute | solution.py:30
  194.8 25.7 %collective-permute-start.30 = (bf16[2,96,576]{2,1,0:T(8,128)(2,1)}, bf16[2,96,576]{2,1,0:T(8,128)(2,1)}, u32[]{:S(2)}, u32[]{:S(2)}) collective-permute-start(bf16[2,96,576]{2,1,0:T(8,128)(2,1)} %fusion.147), channel_id=1, source_target_pairs={{0,8},{4,12},{8,0},{12,4},{16,24},{20,28},{24,16},{28,20},{1,9},{5... | collective-permute-start | bytes 663560 | tf_op jit(solution)/shard_map/ppermute | solution.py:30
  197.6 7.5 %collective-permute-start.35 = (bf16[1,96,576]{2,1,0:T(8,128)(2,1)}, bf16[1,96,576]{2,1,0:T(8,128)(2,1)}, u32[]{:S(2)}, u32[]{:S(2)}) collective-permute-start(bf16[1,96,576]{2,1,0:T(8,128)(2,1)} %fusion.170), channel_id=1, source_target_pairs={{0,16},{4,20},{8,24},{12,28},{16,0},{20,4},{24,8},{28,12},{1,17},{... | collective-permute-start | bytes 331784 | tf_op jit(solution)/shard_map/ppermute | solution.py:30
  201.1 46.3 %all-to-all-start.3 = ((f32[8,24,512]{2,1,0:T(8,128)}), f32[8,24,512]{2,1,0:T(8,128)}, u32[]{:S(2)}, u32[]{:S(2)}) async-start(f32[8,24,512]{2,1,0:T(8,128)} %broadcast_in_dim.22), calls=%async_computation.3 | async-start | bytes 786432 | tf_op jit(solution)/shard_map/all_to_all | solution.py:243
  217.4 23.7 %collective-permute-start.17 = (bf16[4,96,576]{2,1,0:T(8,128)(2,1)}, bf16[4,96,576]{2,1,0:T(8,128)(2,1)}, u32[]{:S(2)}, u32[]{:S(2)}) collective-permute-start(bf16[4,96,576]{2,1,0:T(8,128)(2,1)} %fusion.51), channel_id=1, source_target_pairs={{0,4},{4,0},{8,12},{12,8},{16,20},{20,16},{24,28},{28,24},{1,5},{5... | collective-permute-start | bytes 1327112 | tf_op jit(solution)/shard_map/ppermute | solution.py:30
  225.0 7.9 %collective-permute-start.26 = (bf16[2,96,576]{2,1,0:T(8,128)(2,1)}, bf16[2,96,576]{2,1,0:T(8,128)(2,1)S(1)}, u32[]{:S(2)}, u32[]{:S(2)}) collective-permute-start(bf16[2,96,576]{2,1,0:T(8,128)(2,1)} %fusion.146), channel_id=1, source_target_pairs={{0,8},{4,12},{8,0},{12,4},{16,24},{20,28},{24,16},{28,20},{1,9},{5... | collective-permute-start | bytes 663560 | tf_op jit(solution)/shard_map/ppermute | solution.py:30
  234.8 9.6 %collective-permute-start.22 = (bf16[2,96,576]{2,1,0:T(8,128)(2,1)}, bf16[2,96,576]{2,1,0:T(8,128)(2,1)}, u32[]{:S(2)}, u32[]{:S(2)}) collective-permute-start(bf16[2,96,576]{2,1,0:T(8,128)(2,1)} %fusion.145), channel_id=1, source_target_pairs={{0,8},{4,12},{8,0},{12,4},{16,24},{20,28},{24,16},{28,20},{1,9},{5... | collective-permute-start | bytes 663560 | tf_op jit(solution)/shard_map/ppermute | solution.py:30
  242.3 8.5 %collective-permute-start.18 = (bf16[2,96,576]{2,1,0:T(8,128)(2,1)S(1)}, bf16[2,96,576]{2,1,0:T(8,128)(2,1)S(1)}, u32[]{:S(2)}, u32[]{:S(2)}) collective-permute-start(bf16[2,96,576]{2,1,0:T(8,128)(2,1)S(1)} %fusion.144), channel_id=1, source_target_pairs={{0,8},{4,12},{8,0},{12,4},{16,24},{20,28},{24,16},{28,20},{1,9},{5... | collective-permute-start | bytes 663560 | tf_op jit(solution)/shard_map/ppermute | solution.py:30
  245.5 9.2 %collective-permute-start.23 = (bf16[1,96,576]{2,1,0:T(8,128)(2,1)S(1)}, bf16[1,96,576]{2,1,0:T(8,128)(2,1)S(1)}, u32[]{:S(2)}, u32[]{:S(2)}) collective-permute-start(bf16[1,96,576]{2,1,0:T(8,128)(2,1)S(1)} %fusion.167), channel_id=1, source_target_pairs={{0,16},{4,20},{8,24},{12,28},{16,0},{20,4},{24,8},{28,12},{1,17},{... | collective-permute-start | bytes 331784 | tf_op jit(solution)/shard_map/ppermute | solution.py:30
  (134 other events, 521.1 us)

commit v2 on v1

v2 whole, which is shorter than its diff:
```python
import jax
import jax.numpy as jnp
from jax import lax
from jax.sharding import PartitionSpec as P

LAYERS = 5
WIN = 16
CORES = 2

bf16 = jnp.bfloat16
f32 = jnp.float32


def dilations(shard_rows):
    return (shard_rows // 8, shard_rows // 2, shard_rows, 2 * shard_rows, 4 * shard_rows)


def core_swap(value):
    count = lax.axis_size("ch")
    return lax.ppermute(value, "ch", [(i, i ^ 1) for i in range(count)])


def chip_shift(value, by):
    count = lax.axis_size("ch")
    return lax.ppermute(value, "ch", [(i, (i + CORES * by) % count) for i in range(count)])


def seq_swap(value, bit):
    count = lax.axis_size("seq")
    return lax.ppermute(value, "seq", [(i, i ^ bit) for i in range(count)])


def choose(index, options):
    picked = options[0]
    for place, option in enumerate(options[1:], 1):
        picked = jnp.where(index == place, option, picked)
    return picked


def rolled(field, by):
    if by == 0:
        return field
    blank = jnp.zeros((abs(by),) + field.shape[1:], field.dtype)
    if by > 0:
        return jnp.concatenate([field[by:], blank], axis=0)
    return jnp.concatenate([blank, field[:by]], axis=0)


def chip_scatter_parts(total, chip, chips):
    parts = jnp.split(total, chips, axis=1)
    sends = [choose((chip + by) % chips, parts).astype(bf16) for by in range(1, chips)]
    return choose(chip, parts), sends


def tied(*values):
    return lax.optimization_barrier(values)


def by_strand(strand, own, sibling):
    return [jnp.where(strand == 0, own, sibling), jnp.where(strand == 0, sibling, own)]


def pieces(value):
    high = value.astype(bf16)
    rest = value - high.astype(f32)
    middle = rest.astype(bf16)
    return high, middle, (rest - middle.astype(f32)).astype(bf16)


class BlockSum:
    def __init__(self, kept, sent):
        self.kept, self.sent = kept, sent
        self.bit = 1

    def move(self):
        return seq_swap(self.sent, self.bit)

    def join(self, received):
        total = self.kept + received.astype(f32)
        half = total.shape[0] // 2
        self.bit *= 2
        if self.bit < lax.axis_size("seq"):
            self.kept, self.sent = total[:half], total[half:].astype(bf16)
        else:
            self.kept, self.sent = total, None


def shards(
    genome, stem_weight, dilated_filter_weight, head_weight, window_start, window_track, targets
):
    shard_rows, pool = genome.shape
    seqs = lax.axis_size("seq")
    chips = lax.axis_size("ch") // CORES
    seq = lax.axis_index("seq")
    strand = lax.axis_index("ch") % CORES
    chip = lax.axis_index("ch") // CORES
    spans = dilations(shard_rows)
    classes = spans[0]
    own_classes = classes // seqs
    steps = shard_rows // classes
    reach = tuple(span // classes * own_classes for span in spans)
    quarter = stem_weight.shape[0]
    channels = dilated_filter_weight.shape[3]
    block = channels // seqs
    tracks = head_weight.shape[1]

    blocks = (
        genome.astype(bf16)
        .reshape(steps, seqs, own_classes, pool)
        .transpose(1, 0, 2, 3)
        .reshape(seqs, steps * own_classes, pool)
    )
    blocks = lax.all_to_all(blocks, "seq", 0, 0, tiled=True)

    stem_own = [stem_weight] + [chip_shift(stem_weight, by) for by in range(1, chips)]
    stem_pairs = [
        jnp.concatenate(by_strand(strand, part, core_swap(part))) for part in stem_own
    ]
    stem_full = jnp.concatenate([choose((chip - p) % chips, stem_pairs) for p in range(chips)])

    sibling_filter = core_swap(dilated_filter_weight)

    def filter_of(layer):
        return jnp.concatenate(
            by_strand(strand, dilated_filter_weight[layer], sibling_filter[layer]), axis=1
        )

    bases = blocks.reshape(shard_rows, pool)
    row = jnp.arange(shard_rows, dtype=jnp.int32)
    step_of = row // own_classes
    step_of = jnp.where(strand == 0, step_of, shard_rows // own_classes - 1 - step_of)
    class_of = row % own_classes
    source_row = step_of * own_classes + class_of
    order = (source_row[:, None] == row[None, :]).astype(bf16)
    letter = jnp.arange(4 * pool, dtype=jnp.int32)
    place = jnp.where(strand == 0, letter // 4, pool - 1 - letter // 4)
    spread_place = (jnp.arange(pool, dtype=jnp.int32)[:, None] == place[None, :]).astype(bf16)
    base_of = jnp.where(strand == 0, letter % 4, 3 - letter % 4)
    ordered = jnp.dot(order, bases, preferred_element_type=f32).astype(bf16)
    wide = jnp.dot(ordered, spread_place, preferred_element_type=f32)
    letters = (wide == base_of[None, :].astype(f32)).astype(bf16)
    position = step_of * classes + seq * own_classes + class_of

    member = (
        (position[None, :] >= window_start[:, None])
        & (position[None, :] < window_start[:, None] + WIN)
    ).astype(f32)
    counts = jnp.sum((window_track[:, None] == window_track[None, :]).astype(f32), axis=1)
    at_track = (
        jnp.arange(tracks, dtype=jnp.int32)[None, :] == window_track[:, None]
    ).astype(bf16)

    bits = seqs.bit_length() - 1
    slot = jnp.arange(channels, dtype=jnp.int32) // block
    away = sum(((slot >> (bits - 1 - b)) & 1) << b for b in range(bits))
    wanted = (seq ^ away) * block + jnp.arange(channels, dtype=jnp.int32) % block
    by_distance = (
        jnp.arange(channels, dtype=jnp.int32)[:, None] == wanted[None, :]
    ).astype(bf16)

    whole = lax.dot_general(
        letters, stem_full, (((1,), (1,)), ((), ())), preferred_element_type=f32
    )
    active = jax.nn.gelu(whole).astype(bf16)
    stream = choose(chip, jnp.split(whole, chips, axis=1))
    filters = [filter_of(0)]
    streams = []
    actives = []
    for layer in range(LAYERS):
        streams.append(stream)
        for tap in range(3):
            stream = stream + lax.dot_general(
                rolled(active, (tap - 1) * reach[layer]),
                filters[layer][tap],
                (((1,), (1,)), ((), ())),
                preferred_element_type=f32,
            )
        if layer < LAYERS - 1:
            own = jax.nn.gelu(stream).astype(bf16)
            (own,) = tied(own)
            parts = [chip_shift(own, by) for by in range(1, chips)]
            beside = [
                filter_of(layer + 1),
                jnp.dot(active, by_distance, preferred_element_type=f32).astype(bf16),
            ]
            if layer == 0:
                columns = lax.dot_general(
                    head_weight, at_track, (((1,), (1,)), ((), ())), preferred_element_type=f32
                ).astype(bf16)
                beside.append(columns)
            if layer == 1:
                beside.append(
                    jnp.concatenate(by_strand(strand, columns, core_swap(columns))).astype(f32)
                )
            parts, beside = tied(parts, beside)
            filters.append(beside[0])
            actives.append(beside[1])
            if layer == 0:
                columns = beside[2]
            if layer == 1:
                half_columns = beside[2]
            parts = [own] + list(parts)
            active = jnp.concatenate(
                [choose((chip - p) % chips, parts) for p in range(chips)], axis=1
            )

    pooled = (
        lax.dot_general(
            stream, member, (((0,), (1,)), ((), ())), precision=lax.Precision.HIGHEST
        )
        / WIN
    )
    partial_score = 0.5 * jnp.sum(pooled * half_columns, axis=0)
    everyone = seqs * chips * CORES
    scores = lax.all_to_all(
        jnp.broadcast_to(partial_score, (everyone,) + partial_score.shape),
        ("seq", "ch"),
        0,
        0,
        tiled=True,
    )
    pooled_parts = [pooled[:quarter], pooled[quarter:]]
    pooled_own = choose(strand, pooled_parts) + core_swap(choose(1 - strand, pooled_parts))
    last_active = jnp.dot(active, by_distance, preferred_element_type=f32).astype(bf16)
    scores, pooled_own, last_active = tied(scores, pooled_own, last_active)
    actives.append(last_active)
    window_score = jnp.sum(scores, axis=0)
    loss_slope = (jnp.exp(window_score) - targets) / counts

    weights_back = 0.5 / WIN * loss_slope[None, :] * half_columns
    grad = lax.dot_general(
        member, weights_back, (((0,), (1,)), ((), ())), precision=lax.Precision.HIGHEST
    )
    sums = []
    pooled_bit = 1
    for layer in reversed(range(LAYERS)):
        upstream = grad.astype(bf16)
        taps = [rolled(upstream, (1 - tap) * reach[layer]) for tap in range(3)]
        back = sum(
            jnp.dot(taps[tap], filters[layer][tap], preferred_element_type=f32)
            for tap in range(3)
        )
        mine, sends = chip_scatter_parts(back, chip, chips)
        going = [s for s in sums if s.sent is not None]
        sends, seq_sends, taps = tied(sends, [s.sent for s in going], taps)
        for s, sent in zip(going, seq_sends):
            s.sent = sent
        received = [chip_shift(sent, by) for by, sent in enumerate(sends, 1)]
        seq_received = [s.move() for s in going]
        if pooled_bit < seqs:
            pooled_received = seq_swap(pooled_own, pooled_bit)
            pooled_bit *= 2
        else:
            pooled_received = jnp.zeros_like(pooled_own)
        halves = [
            jnp.concatenate([tap[:, :quarter] for tap in taps], axis=1),
            jnp.concatenate([tap[:, quarter:] for tap in taps], axis=1),
        ]
        theirs = lax.dot_general(
            actives[layer],
            choose(1 - strand, halves),
            (((0,), (0,)), ((), ())),
            preferred_element_type=f32,
        ).astype(bf16)
        theirs = core_swap(theirs)
        ours = choose(strand, halves)
        near, far = jnp.split(actives[layer], 2, axis=1)
        keep = lax.dot_general(
            near, ours, (((0,), (0,)), ((), ())), preferred_element_type=f32
        ) + theirs[: channels // 2].astype(f32)
        send = (
            lax.dot_general(far, ours, (((0,), (0,)), ((), ())), preferred_element_type=f32)
            + theirs[channels // 2 :].astype(f32)
        ).astype(bf16)
        received, seq_received, pooled_received, keep, send = tied(
            received, seq_received, pooled_received, keep, send
        )
        for s, got in zip(going, seq_received):
            s.join(got)
        pooled_own = pooled_own + pooled_received
        sums.append(BlockSum(keep, send))
        through = mine
        for got in received:
            through = through + got.astype(f32)
        pullback = jax.vjp(jax.nn.gelu, streams[layer])[1]
        grad = grad + pullback(through)[0]

    stem_part = lax.dot_general(
        grad.astype(bf16), letters, (((0,), (0,)), ((), ())), preferred_element_type=f32
    )
    stem_parts = [stem_part[:quarter], stem_part[quarter:]]
    stem_own = choose(strand, stem_parts) + core_swap(
        choose(1 - strand, stem_parts).astype(bf16)
    ).astype(f32)
    stem_send = stem_own.astype(bf16).reshape(seqs, quarter // seqs, -1)
    going = [s for s in sums if s.sent is not None]
    seq_received = [s.move() for s in going]
    stem_blocks = lax.all_to_all(stem_send, "seq", 0, 0, tiled=True)
    stem_blocks, seq_received, pooled_own = tied(stem_blocks, seq_received, pooled_own)
    for s, got in zip(going, seq_received):
        s.join(got)
    stem_block = jnp.sum(stem_blocks.astype(f32), axis=0)
    stem_grad = lax.all_to_all(
        jnp.broadcast_to(stem_block, (seqs,) + stem_block.shape), "seq", 0, 0, tiled=True
    ).reshape(quarter, -1)
    while pooled_bit < seqs:
        pooled_own = pooled_own + seq_swap(pooled_own, pooled_bit)
        pooled_bit *= 2
    going = [s for s in sums if s.sent is not None]
    while going:
        for s in going:
            s.join(s.move())
        going = [s for s in sums if s.sent is not None]
    head_grad = lax.dot_general(
        jnp.concatenate(pieces(0.5 * loss_slope[None, :] * pooled_own), axis=1),
        jnp.concatenate([at_track] * 3),
        (((1,), (0,)), ((), ())),
        preferred_element_type=f32,
    )
    conv_grad = jnp.stack(
        [s.kept.reshape(block, 3, quarter).transpose(1, 2, 0) for s in sums[::-1]]
    )
    return (window_score, conv_grad, stem_grad, head_grad)


def solution(mesh):
    return jax.shard_map(
        shards,
        mesh=mesh,
        in_specs=(
            P("seq", None),
            P("ch", None),
            P(None, None, "ch", None),
            P("ch", None),
            P(),
            P(),
            P(),
        ),
        out_specs=(P(), P(None, None, "ch", "seq"), P("ch", None), P("ch", None)),
        check_vma=False,
    )
```

time: 264 us -> 211 us (0.80)
  local copies, waits for them, and re-layouts: 44.1 us -> 12.7 us
  other arithmetic: 51.5 us -> 23.9 us
  waiting for transfers between devices: 58.9 us -> 86.3 us
  starting transfers between devices: 62.8 us -> 45.4 us
    ppermute x18, waiting for transfers between devices: 21.7 us -> 48.3 us  [seq_swap(): return lax.ppermute(value, 'seq', [(i, i ^ bit) for i in range(count)])]
    add x10 -> x0, local copies, waits for them, and re-layouts: 14.5 us -> none  [the longest x5 11.2 us: shards(): ours = filter_part(choose(strand, halves)) + core_swap(theirs).astype(f32)]
    convert_element_type x21 -> x8, other arithmetic: 14.5 us -> 1.03 us  [the longest x1 0.78 us: shards(): stem_send = stem_own.astype(bf16).reshape(seqs, quarter // seqs, -1)]
    unnamed x247 -> x81, local copies, waits for them, and re-layouts: 17.5 us -> 5.13 us
    select_n x9 -> x6, other arithmetic: 9.44 us -> 1.9 us  [choose(): picked = jnp.where(index == place, option, picked)]
    ppermute x10, starting transfers between devices: 14.1 us -> 7.89 us  [chip_shift(): lax.ppermute(value, 'ch', [(i, (i + CORES * by) % count) for i in range(c...]
    ppermute x10, waiting for transfers between devices: 32 us -> 26.1 us  [chip_shift(): lax.ppermute(value, 'ch', [(i, (i + CORES * by) % count) for i in range(c...]
    ppermute x18, starting transfers between devices: 25.9 us -> 20.1 us  [seq_swap(): return lax.ppermute(value, 'seq', [(i, i ^ bit) for i in range(count)])]
  transfers between devices with their start and end apart: 46 -> 43, of which waited for: 16 -> 27; matrix products, arithmetic and copies ran while one was open for 45% -> 20% of each run, Pallas kernels for 0% -> 0%
where the time goes in v2:
time: 211 us; the launch traced here: 210 us
  waiting for transfers between devices  86.3 us (41%)
  starting transfers between devices  45.4 us (22%)
  matrix products  40 us (19%)
  other arithmetic  23.9 us (11%)
  local copies, waits for them, and re-layouts  12.7 us (6%)
    ppermute x18, waiting for transfers between devices, seq_swap(): return lax.ppermute(value, 'seq', [(i, i ^ bit) for i in range(count)])  48.3 us
    ppermute x10, waiting for transfers between devices, chip_shift(): lax.ppermute(value, 'ch', [(i, (i + CORES * by) % count) for i in range(c...  26.1 us
    ppermute x18, starting transfers between devices, seq_swap(): return lax.ppermute(value, 'seq', [(i, i ^ bit) for i in range(count)])  20.1 us
    ppermute x10, starting transfers between devices, chip_shift(): lax.ppermute(value, 'ch', [(i, (i + CORES * by) % count) for i in range(c...  7.89 us
    dot_general x5, matrix products, shards(): jnp.dot(active, by_distance, preferred_element_type=f32).astype(bf16)  7.26 us
    dot_general x15, matrix products, shards(): lax.dot_general(rolled(active, (tap - 1) * reach[layer]), filters[layer][...  6.14 us
    all_to_all x1, starting transfers between devices, shards(): blocks = lax.all_to_all(blocks, 'seq', 0, 0, tiled=True)  5.83 us
    add x15, other arithmetic, join(): total = self.kept + received.astype(f32)  5.82 us
  transfers between devices with their start and end apart: 43, of which 27 were waited for; matrix products, arithmetic and copies ran while one was open for 20% of the time, Pallas kernels for 0%

profile of v2, /device:TPU:0, one launch (start us, length us, event | category | flops | bytes accessed | tf_op | source)
XLA Modules:
  0.0 210.2 jit_solution(16951983324796570284)
XLA Ops:
  1.2 2.6 %collective-permute-start = (bf16[192,512]{1,0:T(8,128)(2,1)}, bf16[192,512]{1,0:T(8,128)(2,1)S(1)}, u32[]{:S(2)}, u32[]{:S(2)}) collective-permute-start(bf16[192,512]{1,0:T(8,128)(2,1)} %param.8), channel_id=1, source_target_pairs={{0,2},{1,3},{2,0},{3,1},{4,6},{5,7},{6,4},{7,5},{8,10},{9,11},{10,... | collective-permute-start | bytes 589832 | tf_op jit(solution)/shard_map/ppermute | solution.py:25
  5.5 5.8 %all-to-all-start = ((bf16[8,32,128]{2,1,0:T(8,128)(2,1)}), bf16[8,32,128]{2,1,0:T(8,128)(2,1)S(1)}, u32[]{:S(2)}, u32[]{:S(2)}) async-start(bf16[8,32,128]{2,1,0:T(8,128)(2,1)} %copy.16), calls=%async_computation | async-start | bytes 131072 | tf_op jit(solution)/shard_map/all_to_all | solution.py:113
  12.1 2.1 fusion.25
  14.9 3.3 %all-to-all-done = bf16[8,32,128]{2,1,0:T(8,128)(2,1)S(1)} async-done(((bf16[8,32,128]{2,1,0:T(8,128)(2,1)}), bf16[8,32,128]{2,1,0:T(8,128)(2,1)S(1)}, u32[]{:S(2)}, u32[]{:S(2)}) %all-to-all-start) | async-done | bytes 65568 | tf_op jit(solution)/shard_map/all_to_all | solution.py:113
  22.5 4.1 %select_bitcast_fusion.1 = (bf16[3,192,768]{2,1,0:T(8,128)(2,1)S(1)}, bf16[3,192,768]{2,1,0:T(8,128)(2,1)S(1)}, bf16[3,192,768]{2,1,0:T(8,128)(2,1)S(1)}, bf16[3...) fusion(pred[]{:T(512)S(6)} %eq.73, ...), kind=kLoop, calls=%fused_computation.87 | loop fusion | flops 3981312 | bytes 16809984 | tf_op jit(solution)/shard_map/jit(_where)/select_n | solution.py:60
  30.5 5.9 %collective-permute-done.4 = bf16[256,384]{1,0:T(8,128)(2,1)S(1)} collective-permute-done((bf16[256,384]{1,0:T(8,128)(2,1)S(1)}, bf16[256,384]{1,0:T(8,128)(2,1)S(1)}, u32[]{:S(2)}, u32[]{:S(2)}) %collective-permute-start.4) | collective-permute-done | bytes 196640 | tf_op jit(solution)/shard_map/ppermute | solution.py:25
  39.8 6.7 %collective-permute-done.5 = bf16[256,384]{1,0:T(8,128)(2,1)S(1)} collective-permute-done((bf16[256,384]{1,0:T(8,128)(2,1)S(1)}, bf16[256,384]{1,0:T(8,128)(2,1)S(1)}, u32[]{:S(2)}, u32[]{:S(2)}) %collective-permute-start.5) | collective-permute-done | bytes 196640 | tf_op jit(solution)/shard_map/ppermute | solution.py:25
  50.0 4.6 %collective-permute-done.7 = bf16[256,384]{1,0:T(8,128)(2,1)S(1)} collective-permute-done((bf16[256,384]{1,0:T(8,128)(2,1)S(1)}, bf16[256,384]{1,0:T(8,128)(2,1)S(1)}, u32[]{:S(2)}, u32[]{:S(2)}) %collective-permute-start.7) | collective-permute-done | bytes 196640 | tf_op jit(solution)/shard_map/ppermute | solution.py:25
  58.1 3.6 %collective-permute-done.8 = bf16[256,384]{1,0:T(8,128)(2,1)S(1)} collective-permute-done((bf16[256,384]{1,0:T(8,128)(2,1)S(1)}, bf16[256,384]{1,0:T(8,128)(2,1)S(1)}, u32[]{:S(2)}, u32[]{:S(2)}) %collective-permute-start.8) | collective-permute-done | bytes 196640 | tf_op jit(solution)/shard_map/ppermute | solution.py:25
  65.7 1.6 slice_select_fusion.2
  67.9 2.7 %all-to-all-start.1 = ((f32[32,1,128]{2,1,0:T(1,128)}), f32[32,1,128]{2,1,0:T(1,128)S(1)}, u32[]{:S(2)}, u32[]{:S(2)}) async-start(f32[32,1,128]{2,1,0:T(1,128)} %broadcast_in_dim.4), calls=%async_computation.1 | async-start | bytes 32768 | tf_op jit(solution)/shard_map/all_to_all | solution.py:215
  70.7 1.6 select_add_fusion
  72.3 5.3 %all-to-all-done.1 = f32[32,1,128]{2,1,0:T(1,128)S(1)} async-done(((f32[32,1,128]{2,1,0:T(1,128)}), f32[32,1,128]{2,1,0:T(1,128)S(1)}, u32[]{:S(2)}, u32[]{:S(2)}) %all-to-all-start.1) | async-done | bytes 16416 | tf_op jit(solution)/shard_map/all_to_all | solution.py:215
  86.2 2.0 collective-permute-done.11
  88.2 1.9 collective-permute-done.10
  96.3 1.8 collective-permute-done.15
  98.2 2.7 %collective-permute-done.13 = bf16[256,384]{1,0:T(8,128)(2,1)S(1)} collective-permute-done((bf16[256,384]{1,0:T(8,128)(2,1)S(1)}, bf16[256,384]{1,0:T(8,128)(2,1)S(1)}, u32[]{:S(2)}, u32[]{:S(2)}) %collective-permute-start.13) | collective-permute-done | bytes 196640 | tf_op jit(solution)/shard_map/ppermute | solution.py:25
  100.8 5.0 %collective-permute-done.14 = bf16[384,576]{0,1:T(8,128)(2,1)S(1)} collective-permute-done((bf16[384,576]{0,1:T(8,128)(2,1)S(1)}, bf16[384,576]{0,1:T(8,128)(2,1)S(1)}, u32[]{:S(2)}, u32[]{:S(2)}) %collective-permute-start.14) | collective-permute-done | bytes 442400 | tf_op jit(solution)/shard_map/ppermute | solution.py:30
  113.2 4.1 %collective-permute-done.20 = f32[192,128]{1,0:T(8,128)S(1)} collective-permute-done((f32[192,128]{1,0:T(8,128)S(1)}, f32[192,128]{1,0:T(8,128)S(1)}, u32[]{:S(2)}, u32[]{:S(2)}) %collective-permute-start.20) | collective-permute-done | bytes 98336 | tf_op jit(solution)/shard_map/ppermute | solution.py:30
  118.0 3.0 %collective-permute-done.18 = bf16[192,576]{0,1:T(8,128)(2,1)S(1)} collective-permute-done((bf16[192,576]{0,1:T(8,128)(2,1)S(1)}, bf16[192,576]{0,1:T(8,128)(2,1)S(1)}, u32[]{:S(2)}, u32[]{:S(2)}) %collective-permute-start.18) | collective-permute-done | bytes 221216 | tf_op jit(solution)/shard_map/ppermute | solution.py:30
  127.8 2.4 %collective-permute-start.23 = (bf16[96,576]{0,1:T(8,128)(2,1)S(1)}, bf16[96,576]{0,1:T(8,128)(2,1)S(1)}, u32[]{:S(2)}, u32[]{:S(2)}) collective-permute-start(bf16[96,576]{0,1:T(8,128)(2,1)S(1)} %slice.767), channel_id=1, source_target_pairs={{0,16},{4,20},{8,24},{12,28},{16,0},{20,4},{24,8},{28,12},{1,17},{... | collective-permute-start | bytes 331784 | tf_op jit(solution)/shard_map/ppermute | solution.py:30
  131.2 5.7 %collective-permute-done.23 = bf16[96,576]{0,1:T(8,128)(2,1)S(1)} collective-permute-done((bf16[96,576]{0,1:T(8,128)(2,1)S(1)}, bf16[96,576]{0,1:T(8,128)(2,1)S(1)}, u32[]{:S(2)}, u32[]{:S(2)}) %collective-permute-start.23) | collective-permute-done | bytes 110624 | tf_op jit(solution)/shard_map/ppermute | solution.py:30
  144.4 2.4 %collective-permute-start.29 = (bf16[192,576]{0,1:T(8,128)(2,1)S(1)}, bf16[192,576]{0,1:T(8,128)(2,1)S(1)}, u32[]{:S(2)}, u32[]{:S(2)}) collective-permute-start(bf16[192,576]{0,1:T(8,128)(2,1)S(1)} %slice.760), channel_id=1, source_target_pairs={{0,8},{4,12},{8,0},{12,4},{16,24},{20,28},{24,16},{28,20},{1,9},{5... | collective-permute-start | bytes 663560 | tf_op jit(solution)/shard_map/ppermute | solution.py:30
  151.5 5.1 %collective-permute-done.28 = bf16[96,576]{0,1:T(8,128)(2,1)S(1)} collective-permute-done((bf16[96,576]{0,1:T(8,128)(2,1)S(1)}, bf16[96,576]{0,1:T(8,128)(2,1)S(1)}, u32[]{:S(2)}, u32[]{:S(2)}) %collective-permute-start.28) | collective-permute-done | bytes 110624 | tf_op jit(solution)/shard_map/ppermute | solution.py:30
  158.3 1.8 collective-permute-start.34
  163.9 3.7 %all-to-all-start.2 = ((bf16[8,24,512]{2,1,0:T(8,128)(2,1)}), bf16[8,24,512]{2,1,0:T(8,128)(2,1)S(1)}, u32[]{:S(2)}, u32[]{:S(2)}) async-start(bf16[8,24,512]{2,1,0:T(8,128)(2,1)} %bitcast.31), calls=%async_computation.2 | async-start | bytes 393216 | tf_op jit(solution)/shard_map/all_to_all | solution.py:298
  170.7 6.2 %collective-permute-done.35 = bf16[384,576]{0,1:T(8,128)(2,1)} collective-permute-done((bf16[384,576]{0,1:T(8,128)(2,1)}, bf16[384,576]{0,1:T(8,128)(2,1)}, u32[]{:S(2)}, u32[]{:S(2)}) %collective-permute-start.35) | collective-permute-done | bytes 442400 | tf_op jit(solution)/shard_map/ppermute | solution.py:30
  178.2 1.6 collective-permute-start.38
  183.2 3.8 %all-to-all-start.3 = ((f32[8,24,512]{2,1,0:T(8,128)}), f32[8,24,512]{2,1,0:T(8,128)S(1)}, u32[]{:S(2)}, u32[]{:S(2)}) async-start(f32[8,24,512]{2,1,0:T(8,128)} %broadcast_in_dim.5), calls=%async_computation.3 | async-start | bytes 786432 | tf_op jit(solution)/shard_map/all_to_all | solution.py:303
  187.1 4.8 %fusion = f32[192,5313]{1,0:T(8,128)} fusion(pred[128,5313]{1,0:T(32,128)(4,1)} %iota_compare_fusion, bf16[192,128]{1,0:T(8,128)(2,1)S(1)} %get-tuple-element.248, bf16[192,128]{1,0:T(8,128)(2,1)S(1)} %get-tuple-element.249, bf16[192,128]{1,0:T(8,128)(2,1)S(1)} %get-tuple-element.247), kind=kOutput, calls=%fused_computation | convolution fusion | flops 787956480 | bytes 4907904 | tf_op jit(solution)/shard_map/dot_general | solution.py:314
  191.9 6.0 %collective-permute-done.36 = bf16[192,576]{0,1:T(8,128)(2,1)} collective-permute-done((bf16[192,576]{0,1:T(8,128)(2,1)}, bf16[192,576]{0,1:T(8,128)(2,1)}, u32[]{:S(2)}, u32[]{:S(2)}) %collective-permute-start.36) | collective-permute-done | bytes 221216 | tf_op jit(solution)/shard_map/ppermute | solution.py:30
  200.1 5.7 %collective-permute-done.37 = bf16[96,576]{0,1:T(8,128)(2,1)S(1)} collective-permute-done((bf16[96,576]{0,1:T(8,128)(2,1)S(1)}, bf16[96,576]{0,1:T(8,128)(2,1)S(1)}, u32[]{:S(2)}, u32[]{:S(2)}) %collective-permute-start.37) | collective-permute-done | bytes 110624 | tf_op jit(solution)/shard_map/ppermute | solution.py:30
  (303 shorter events, 88.7 us)
Async XLA Ops:
  0.6 21.8 %collective-permute-start.3 = (bf16[5,3,192,768]{3,2,1,0:T(8,128)(2,1)}, bf16[5,3,192,768]{3,2,1,0:T(8,128)(2,1)}, u32[]{:S(2)}, u32[]{:S(2)}) collective-permute-start(bf16[5,3,192,768]{3,2,1,0:T(8,128)(2,1)} %param.9), channel_id=1, source_target_pairs={{0,1},{1,0},{2,3},{3,2},{4,5},{5,4},{6,7},{7,6},{8,9},{9,8},{10,11... | collective-permute-start | bytes 13271048 | tf_op jit(solution)/shard_map/ppermute | solution.py:20
  1.2 17.5 %collective-permute-start = (bf16[192,512]{1,0:T(8,128)(2,1)}, bf16[192,512]{1,0:T(8,128)(2,1)S(1)}, u32[]{:S(2)}, u32[]{:S(2)}) collective-permute-start(bf16[192,512]{1,0:T(8,128)(2,1)} %param.8), channel_id=1, source_target_pairs={{0,2},{1,3},{2,0},{3,1},{4,6},{5,7},{6,4},{7,5},{8,10},{9,11},{10,... | collective-permute-start | bytes 589832 | tf_op jit(solution)/shard_map/ppermute | solution.py:25
  3.7 15.0 %collective-permute-start.2 = (bf16[192,512]{1,0:T(8,128)(2,1)}, bf16[192,512]{1,0:T(8,128)(2,1)S(1)}, u32[]{:S(2)}, u32[]{:S(2)}) collective-permute-start(bf16[192,512]{1,0:T(8,128)(2,1)} %param.8), channel_id=1, source_target_pairs={{0,1},{1,0},{2,3},{3,2},{4,5},{5,4},{6,7},{7,6},{8,9},{9,8},{10,11... | collective-permute-start | bytes 589832 | tf_op jit(solution)/shard_map/ppermute | solution.py:20
  5.5 12.7 %all-to-all-start = ((bf16[8,32,128]{2,1,0:T(8,128)(2,1)}), bf16[8,32,128]{2,1,0:T(8,128)(2,1)S(1)}, u32[]{:S(2)}, u32[]{:S(2)}) async-start(bf16[8,32,128]{2,1,0:T(8,128)(2,1)} %copy.16), calls=%async_computation | async-start | bytes 131072 | tf_op jit(solution)/shard_map/all_to_all | solution.py:113
  29.4 7.0 %collective-permute-start.4 = (bf16[256,384]{1,0:T(8,128)(2,1)S(1)}, bf16[256,384]{1,0:T(8,128)(2,1)S(1)}, u32[]{:S(2)}, u32[]{:S(2)}) collective-permute-start(bf16[256,384]{1,0:T(8,128)(2,1)S(1)} %get-tuple-element.254), channel_id=1, source_target_pairs={{0,2},{1,3},{2,0},{3,1},{4,6},{5,7},{6,4},{7,5},{8,10},{9,11},{10,... | collective-permute-start | bytes 589832 | tf_op jit(solution)/shard_map/ppermute | solution.py:25
  39.2 7.3 %collective-permute-start.5 = (bf16[256,384]{1,0:T(8,128)(2,1)S(1)}, bf16[256,384]{1,0:T(8,128)(2,1)S(1)}, u32[]{:S(2)}, u32[]{:S(2)}) collective-permute-start(bf16[256,384]{1,0:T(8,128)(2,1)S(1)} %get-tuple-element.256), channel_id=1, source_target_pairs={{0,2},{1,3},{2,0},{3,1},{4,6},{5,7},{6,4},{7,5},{8,10},{9,11},{10,... | collective-permute-start | bytes 589832 | tf_op jit(solution)/shard_map/ppermute | solution.py:25
  48.0 6.6 %collective-permute-start.7 = (bf16[256,384]{1,0:T(8,128)(2,1)S(1)}, bf16[256,384]{1,0:T(8,128)(2,1)S(1)}, u32[]{:S(2)}, u32[]{:S(2)}) collective-permute-start(bf16[256,384]{1,0:T(8,128)(2,1)S(1)} %get-tuple-element.258), channel_id=1, source_target_pairs={{0,2},{1,3},{2,0},{3,1},{4,6},{5,7},{6,4},{7,5},{8,10},{9,11},{10,... | collective-permute-start | bytes 589832 | tf_op jit(solution)/shard_map/ppermute | solution.py:25
  67.9 9.7 %all-to-all-start.1 = ((f32[32,1,128]{2,1,0:T(1,128)}), f32[32,1,128]{2,1,0:T(1,128)S(1)}, u32[]{:S(2)}, u32[]{:S(2)}) async-start(f32[32,1,128]{2,1,0:T(1,128)} %broadcast_in_dim.4), calls=%async_computation.1 | async-start | bytes 32768 | tf_op jit(solution)/shard_map/all_to_all | solution.py:215
  82.7 7.3 %collective-permute-start.10 = (bf16[256,384]{1,0:T(8,128)(2,1)S(1)}, bf16[256,384]{1,0:T(8,128)(2,1)S(1)}, u32[]{:S(2)}, u32[]{:S(2)}) collective-permute-start(bf16[256,384]{1,0:T(8,128)(2,1)S(1)} %select_convert_fusion.5), channel_id=1, source_target_pairs={{0,2},{1,3},{2,0},{3,1},{4,6},{5,7},{6,4},{7,5},{8,10},{9,11},{10,... | collective-permute-start | bytes 589832 | tf_op jit(solution)/shard_map/ppermute | solution.py:25
  93.5 12.3 %collective-permute-start.14 = (bf16[384,576]{0,1:T(8,128)(2,1)S(1)}, bf16[384,576]{0,1:T(8,128)(2,1)S(1)}, u32[]{:S(2)}, u32[]{:S(2)}) collective-permute-start(bf16[384,576]{0,1:T(8,128)(2,1)S(1)} %add_convert_fusion), channel_id=1, source_target_pairs={{0,4},{4,0},{8,12},{12,8},{16,20},{20,16},{24,28},{28,24},{1,5},{5... | collective-permute-start | bytes 1327112 | tf_op jit(solution)/shard_map/ppermute | solution.py:30
  94.1 6.7 %collective-permute-start.13 = (bf16[256,384]{1,0:T(8,128)(2,1)S(1)}, bf16[256,384]{1,0:T(8,128)(2,1)S(1)}, u32[]{:S(2)}, u32[]{:S(2)}) collective-permute-start(bf16[256,384]{1,0:T(8,128)(2,1)S(1)} %select_convert_fusion.4), channel_id=1, source_target_pairs={{0,2},{1,3},{2,0},{3,1},{4,6},{5,7},{6,4},{7,5},{8,10},{9,11},{10,... | collective-permute-start | bytes 589832 | tf_op jit(solution)/shard_map/ppermute | solution.py:25
  108.9 8.4 %collective-permute-start.20 = (f32[192,128]{1,0:T(8,128)S(1)}, f32[192,128]{1,0:T(8,128)S(1)}, u32[]{:S(2)}, u32[]{:S(2)}) collective-permute-start(f32[192,128]{1,0:T(8,128)S(1)} %add.498), channel_id=1, source_target_pairs={{0,16},{4,20},{8,24},{12,28},{16,0},{20,4},{24,8},{28,12},{1,17},{... | collective-permute-start | bytes 294920 | tf_op jit(solution)/shard_map/ppermute | solution.py:30
  109.5 12.3 %collective-permute-start.19 = (bf16[384,576]{0,1:T(8,128)(2,1)S(1)}, bf16[384,576]{0,1:T(8,128)(2,1)S(1)}, u32[]{:S(2)}, u32[]{:S(2)}) collective-permute-start(bf16[384,576]{0,1:T(8,128)(2,1)S(1)} %fusion.11), channel_id=1, source_target_pairs={{0,4},{4,0},{8,12},{12,8},{16,20},{20,16},{24,28},{28,24},{1,5},{5... | collective-permute-start | bytes 1327112 | tf_op jit(solution)/shard_map/ppermute | solution.py:30
  110.0 11.0 %collective-permute-start.18 = (bf16[192,576]{0,1:T(8,128)(2,1)S(1)}, bf16[192,576]{0,1:T(8,128)(2,1)S(1)}, u32[]{:S(2)}, u32[]{:S(2)}) collective-permute-start(bf16[192,576]{0,1:T(8,128)(2,1)S(1)} %slice.762), channel_id=1, source_target_pairs={{0,8},{4,12},{8,0},{12,4},{16,24},{20,28},{24,16},{28,20},{1,9},{5... | collective-permute-start | bytes 663560 | tf_op jit(solution)/shard_map/ppermute | solution.py:30
  111.6 6.5 %collective-permute-start.17 = (bf16[256,384]{1,0:T(8,128)(2,1)S(1)}, bf16[256,384]{1,0:T(8,128)(2,1)S(1)}, u32[]{:S(2)}, u32[]{:S(2)}) collective-permute-start(bf16[256,384]{1,0:T(8,128)(2,1)S(1)} %select_convert_fusion.3), channel_id=1, source_target_pairs={{0,2},{1,3},{2,0},{3,1},{4,6},{5,7},{6,4},{7,5},{8,10},{9,11},{10,... | collective-permute-start | bytes 589832 | tf_op jit(solution)/shard_map/ppermute | solution.py:25
  125.1 12.8 %collective-permute-start.25 = (bf16[384,576]{0,1:T(8,128)(2,1)S(1)}, bf16[384,576]{0,1:T(8,128)(2,1)S(1)}, u32[]{:S(2)}, u32[]{:S(2)}) collective-permute-start(bf16[384,576]{0,1:T(8,128)(2,1)S(1)} %fusion.12), channel_id=1, source_target_pairs={{0,4},{4,0},{8,12},{12,8},{16,20},{20,16},{24,28},{28,24},{1,5},{5... | collective-permute-start | bytes 1327112 | tf_op jit(solution)/shard_map/ppermute | solution.py:30
  125.7 12.2 %collective-permute-start.24 = (bf16[192,576]{0,1:T(8,128)(2,1)S(1)}, bf16[192,576]{0,1:T(8,128)(2,1)S(1)}, u32[]{:S(2)}, u32[]{:S(2)}) collective-permute-start(bf16[192,576]{0,1:T(8,128)(2,1)S(1)} %slice.761), channel_id=1, source_target_pairs={{0,8},{4,12},{8,0},{12,4},{16,24},{20,28},{24,16},{28,20},{1,9},{5... | collective-permute-start | bytes 663560 | tf_op jit(solution)/shard_map/ppermute | solution.py:30
  127.2 9.8 %collective-permute-start.22 = (bf16[256,384]{1,0:T(8,128)(2,1)S(1)}, bf16[256,384]{1,0:T(8,128)(2,1)S(1)}, u32[]{:S(2)}, u32[]{:S(2)}) collective-permute-start(bf16[256,384]{1,0:T(8,128)(2,1)S(1)} %select_convert_fusion.2), channel_id=1, source_target_pairs={{0,2},{1,3},{2,0},{3,1},{4,6},{5,7},{6,4},{7,5},{8,10},{9,11},{10,... | collective-permute-start | bytes 589832 | tf_op jit(solution)/shard_map/ppermute | solution.py:25
  127.8 9.2 %collective-permute-start.23 = (bf16[96,576]{0,1:T(8,128)(2,1)S(1)}, bf16[96,576]{0,1:T(8,128)(2,1)S(1)}, u32[]{:S(2)}, u32[]{:S(2)}) collective-permute-start(bf16[96,576]{0,1:T(8,128)(2,1)S(1)} %slice.767), channel_id=1, source_target_pairs={{0,16},{4,20},{8,24},{12,28},{16,0},{20,4},{24,8},{28,12},{1,17},{... | collective-permute-start | bytes 331784 | tf_op jit(solution)/shard_map/ppermute | solution.py:30
  141.5 7.3 %collective-permute-start.31 = (bf16[768,576]{0,1:T(8,128)(2,1)S(1)}, bf16[768,576]{0,1:T(8,128)(2,1)S(1)}, u32[]{:S(2)}, u32[]{:S(2)}) collective-permute-start(bf16[768,576]{0,1:T(8,128)(2,1)S(1)} %convolution_convert_fusion), channel_id=1, source_target_pairs={{0,1},{1,0},{2,3},{3,2},{4,5},{5,4},{6,7},{7,6},{8,9},{9,8},{10,11... | collective-permute-start | bytes 2654216 | tf_op jit(solution)/shard_map/ppermute | solution.py:20
  142.9 14.5 %collective-permute-start.30 = (bf16[384,576]{0,1:T(8,128)(2,1)S(1)}, bf16[384,576]{0,1:T(8,128)(2,1)S(1)}, u32[]{:S(2)}, u32[]{:S(2)}) collective-permute-start(bf16[384,576]{0,1:T(8,128)(2,1)S(1)} %fusion.13), channel_id=1, source_target_pairs={{0,4},{4,0},{8,12},{12,8},{16,20},{20,16},{24,28},{28,24},{1,5},{5... | collective-permute-start | bytes 1327112 | tf_op jit(solution)/shard_map/ppermute | solution.py:30
  144.4 12.9 %collective-permute-start.29 = (bf16[192,576]{0,1:T(8,128)(2,1)S(1)}, bf16[192,576]{0,1:T(8,128)(2,1)S(1)}, u32[]{:S(2)}, u32[]{:S(2)}) collective-permute-start(bf16[192,576]{0,1:T(8,128)(2,1)S(1)} %slice.760), channel_id=1, source_target_pairs={{0,8},{4,12},{8,0},{12,4},{16,24},{20,28},{24,16},{28,20},{1,9},{5... | collective-permute-start | bytes 663560 | tf_op jit(solution)/shard_map/ppermute | solution.py:30
  146.8 9.8 %collective-permute-start.27 = (bf16[256,384]{1,0:T(8,128)(2,1)S(1)}, bf16[256,384]{1,0:T(8,128)(2,1)S(1)}, u32[]{:S(2)}, u32[]{:S(2)}) collective-permute-start(bf16[256,384]{1,0:T(8,128)(2,1)S(1)} %select_convert_fusion.1), channel_id=1, source_target_pairs={{0,2},{1,3},{2,0},{3,1},{4,6},{5,7},{6,4},{7,5},{8,10},{9,11},{10,... | collective-permute-start | bytes 589832 | tf_op jit(solution)/shard_map/ppermute | solution.py:25
  147.4 9.3 %collective-permute-start.28 = (bf16[96,576]{0,1:T(8,128)(2,1)S(1)}, bf16[96,576]{0,1:T(8,128)(2,1)S(1)}, u32[]{:S(2)}, u32[]{:S(2)}) collective-permute-start(bf16[96,576]{0,1:T(8,128)(2,1)S(1)} %slice.766), channel_id=1, source_target_pairs={{0,16},{4,20},{8,24},{12,28},{16,0},{20,4},{24,8},{28,12},{1,17},{... | collective-permute-start | bytes 331784 | tf_op jit(solution)/shard_map/ppermute | solution.py:30
  158.3 12.4 %collective-permute-start.34 = (bf16[192,576]{0,1:T(8,128)(2,1)}, bf16[192,576]{0,1:T(8,128)(2,1)}, u32[]{:S(2)}, u32[]{:S(2)}) collective-permute-start(bf16[192,576]{0,1:T(8,128)(2,1)} %slice.759), channel_id=1, source_target_pairs={{0,8},{4,12},{8,0},{12,4},{16,24},{20,28},{24,16},{28,20},{1,9},{5... | collective-permute-start | bytes 663560 | tf_op jit(solution)/shard_map/ppermute | solution.py:30
  161.1 9.7 %collective-permute-start.33 = (bf16[96,576]{0,1:T(8,128)(2,1)S(1)}, bf16[96,576]{0,1:T(8,128)(2,1)S(1)}, u32[]{:S(2)}, u32[]{:S(2)}) collective-permute-start(bf16[96,576]{0,1:T(8,128)(2,1)S(1)} %slice.765), channel_id=1, source_target_pairs={{0,16},{4,20},{8,24},{12,28},{16,0},{20,4},{24,8},{28,12},{1,17},{... | collective-permute-start | bytes 331784 | tf_op jit(solution)/shard_map/ppermute | solution.py:30
  162.5 14.4 %collective-permute-start.35 = (bf16[384,576]{0,1:T(8,128)(2,1)}, bf16[384,576]{0,1:T(8,128)(2,1)}, u32[]{:S(2)}, u32[]{:S(2)}) collective-permute-start(bf16[384,576]{0,1:T(8,128)(2,1)} %fusion.14), channel_id=1, source_target_pairs={{0,4},{4,0},{8,12},{12,8},{16,20},{20,16},{24,28},{28,24},{1,5},{5... | collective-permute-start | bytes 1327112 | tf_op jit(solution)/shard_map/ppermute | solution.py:30
  163.9 13.3 %all-to-all-start.2 = ((bf16[8,24,512]{2,1,0:T(8,128)(2,1)}), bf16[8,24,512]{2,1,0:T(8,128)(2,1)S(1)}, u32[]{:S(2)}, u32[]{:S(2)}) async-start(bf16[8,24,512]{2,1,0:T(8,128)(2,1)} %bitcast.31), calls=%async_computation.2 | async-start | bytes 393216 | tf_op jit(solution)/shard_map/all_to_all | solution.py:298
  178.2 20.9 %collective-permute-start.38 = (bf16[96,576]{0,1:T(8,128)(2,1)S(1)}, bf16[96,576]{0,1:T(8,128)(2,1)}, u32[]{:S(2)}, u32[]{:S(2)}) collective-permute-start(bf16[96,576]{0,1:T(8,128)(2,1)S(1)} %slice.763), channel_id=1, source_target_pairs={{0,16},{4,20},{8,24},{12,28},{16,0},{20,4},{24,8},{28,12},{1,17},{... | collective-permute-start | bytes 331784 | tf_op jit(solution)/shard_map/ppermute | solution.py:30
  182.1 15.8 %collective-permute-start.36 = (bf16[192,576]{0,1:T(8,128)(2,1)}, bf16[192,576]{0,1:T(8,128)(2,1)}, u32[]{:S(2)}, u32[]{:S(2)}) collective-permute-start(bf16[192,576]{0,1:T(8,128)(2,1)} %slice.758), channel_id=1, source_target_pairs={{0,8},{4,12},{8,0},{12,4},{16,24},{20,28},{24,16},{28,20},{1,9},{5... | collective-permute-start | bytes 663560 | tf_op jit(solution)/shard_map/ppermute | solution.py:30
  183.2 26.3 %all-to-all-start.3 = ((f32[8,24,512]{2,1,0:T(8,128)}), f32[8,24,512]{2,1,0:T(8,128)S(1)}, u32[]{:S(2)}, u32[]{:S(2)}) async-start(f32[8,24,512]{2,1,0:T(8,128)} %broadcast_in_dim.5), calls=%async_computation.3 | async-start | bytes 786432 | tf_op jit(solution)/shard_map/all_to_all | solution.py:303
  199.0 6.8 %collective-permute-start.37 = (bf16[96,576]{0,1:T(8,128)(2,1)S(1)}, bf16[96,576]{0,1:T(8,128)(2,1)S(1)}, u32[]{:S(2)}, u32[]{:S(2)}) collective-permute-start(bf16[96,576]{0,1:T(8,128)(2,1)S(1)} %slice.764), channel_id=1, source_target_pairs={{0,16},{4,20},{8,24},{12,28},{16,0},{20,4},{24,8},{28,12},{1,17},{... | collective-permute-start | bytes 331784 | tf_op jit(solution)/shard_map/ppermute | solution.py:30
  (49 other events, 397.1 us)
